TPU v7x, 256 devices: a whole 4x4x8 slice. The times are simulated.
256 devices in a mesh: dp: 32 (over x, z), tensor: 8 (over y, core).
Axes of the slice: x: 4, y: 4, z: 8, core: 2. Of those that a mesh axis runs over, the one named last changes fastest.
Arguments:
- tokens: bfloat16 [1024, 6144], P('dp', 'tensor'), may hold values from -32 to 32
- gain_in: float32 [6144], P('tensor'), may hold values from 0.1 to 1.9
- shift_in: float32 [6144], P('tensor'), may hold values from -3 to 3
- up_weight: bfloat16 [6144, 24576], P('tensor', 'dp'), may hold values from -0.078125 to 0.078125
- up_bias: float32 [24576], P('dp'), may hold values from -3 to 3
- down_weight: bfloat16 [24576, 6144], P('dp', 'tensor'), may hold values from -1 to 1
- gain_out: float32 [6144], P('tensor'), may hold values from 0.1 to 1.9
- curvature: float32 [1024, 6144], P('dp', 'tensor'), may hold values from 0.5 to 12
- up_tangent: bfloat16 [6144, 24576], P('tensor', 'dp'), may hold values from -0.078125 to 0.078125
- down_tangent: bfloat16 [24576, 6144], P('dp', 'tensor'), may hold values from -1 to 1
Outputs:
- up_product: float32 [6144, 24576], P('tensor', 'dp')
- down_product: float32 [24576, 6144], P('dp', 'tensor')
All inputs are finite; a program needn't handle non-finite values.
Results may differ from a plain program's by a relative error of at most 0.003.
Values may be sent and summed in bfloat16 or wider, within the bound.
A program may use at most 128 MiB of HBM per device.

v0:
```python
import jax
import jax.numpy as jnp
from jax import lax
from jax.sharding import PartitionSpec as P

D = 6144


epsilon = 1e-05
root_half = 0.7071067811865476
inv_root_two_pi = 0.3989422804014327


def gelu_value(values):
    return 0.5 * values * (1.0 + lax.erf(values * root_half))


def gelu_slope(values):
    return (
        0.5 * (1.0 + lax.erf(values * root_half))
        + values * jnp.exp(-0.5 * values * values) * inv_root_two_pi
    )


def row_total(values):
    return jnp.sum(values, axis=1)


def on_device(
    tokens,
    gain_in,
    shift_in,
    up_weight,
    up_bias,
    down_weight,
    gain_out,
    curvature,
    up_tangent,
    down_tangent,
):
    model_width = float(D)
    source = tokens.astype(jnp.float32)
    sum_in, square_in = lax.psum((row_total(source), row_total(source * source)), "tensor")
    center_in = sum_in / model_width
    spread_in = square_in / model_width - center_in * center_in
    inverse_in = lax.rsqrt(spread_in + epsilon)[:, None]
    normed = ((source - center_in[:, None]) * inverse_in * gain_in + shift_in).astype(jnp.bfloat16)
    all_normed = lax.all_gather(normed, "dp", axis=0, tiled=True)
    pre_part = jnp.dot(all_normed, up_weight, preferred_element_type=jnp.float32)
    tangent_part = jnp.dot(all_normed, up_tangent, preferred_element_type=jnp.float32)
    share_rows = all_normed.shape[0] // lax.axis_size("tensor")
    pre_total, tangent_total = lax.psum((pre_part, tangent_part), "tensor")
    pre_full = pre_total + up_bias
    slope_full = gelu_slope(pre_full)
    hidden = gelu_value(pre_full).astype(jnp.bfloat16)
    hidden_tangent = (slope_full * tangent_total).astype(jnp.bfloat16)
    slope_rows = lax.dynamic_slice_in_dim(
        slope_full, lax.axis_index("tensor") * share_rows, share_rows, 0
    )
    slope_kept = lax.optimization_barrier(slope_rows.astype(jnp.bfloat16))
    primal = jnp.dot(hidden, down_weight, preferred_element_type=jnp.float32)
    tangent = jnp.dot(hidden_tangent, down_weight, preferred_element_type=jnp.float32) + jnp.dot(
        hidden, down_tangent, preferred_element_type=jnp.float32
    )
    both_outputs = lax.psum_scatter(
        jnp.concatenate([primal, tangent], axis=1), "dp", scatter_dimension=0, tiled=True
    )
    local_width = down_weight.shape[1]
    output = source + both_outputs[:, :local_width]
    output_tangent = both_outputs[:, local_width:]
    factor = gain_out * gain_out * curvature
    sum_out, square_out = lax.psum((row_total(output), row_total(output * output)), "tensor")
    center_out = sum_out / model_width
    inverse_out = lax.rsqrt(square_out / model_width - center_out * center_out + epsilon)[:, None]
    normal_out = (output - center_out[:, None]) * inverse_out
    tangent_sum, tangent_dot = lax.psum(
        (row_total(output_tangent), row_total(normal_out * output_tangent)), "tensor"
    )
    normal_tangent = (
        output_tangent
        - (tangent_sum / model_width)[:, None]
        - normal_out * (tangent_dot / model_width)[:, None]
    ) * inverse_out
    weighted = factor * normal_tangent
    weight_sum, weight_dot = lax.psum(
        (row_total(weighted), row_total(normal_out * weighted)), "tensor"
    )
    cotangent = (
        (
            weighted
            - (weight_sum / model_width)[:, None]
            - normal_out * (weight_dot / model_width)[:, None]
        )
        * inverse_out
    ).astype(jnp.bfloat16)
    all_cotangent = lax.all_gather(cotangent, "dp", axis=0, tiled=True)
    back_part = lax.dot_general(
        all_cotangent, down_weight, (((1,), (1,)), ((), ())), preferred_element_type=jnp.float32
    )
    down_product = lax.dot_general(
        hidden, all_cotangent, (((0,), (0,)), ((), ())), preferred_element_type=jnp.float32
    )
    back_share = lax.psum_scatter(back_part, "tensor", scatter_dimension=0, tiled=True)
    grad_share = (back_share * slope_kept.astype(jnp.float32)).astype(jnp.bfloat16)
    grad_pre = lax.all_gather(grad_share, "tensor", axis=0, tiled=True)
    up_product = lax.dot_general(
        all_normed, grad_pre, (((0,), (0,)), ((), ())), preferred_element_type=jnp.float32
    )
    return (up_product, down_product)


def solution(mesh):
    return jax.shard_map(
        on_device,
        mesh=mesh,
        in_specs=(
            P("dp", "tensor"),
            P("tensor"),
            P("tensor"),
            P("tensor", "dp"),
            P("dp"),
            P("dp", "tensor"),
            P("tensor"),
            P("dp", "tensor"),
            P("tensor", "dp"),
            P("dp", "tensor"),
        ),
        out_specs=(P("tensor", "dp"), P("dp", "tensor")),
        check_vma=False,
    )
```

profile of v0, /device:TPU:1, one launch (start us, length us, event | category | flops | bytes accessed | tf_op | source)
XLA Modules:
  0.0 637.0 jit_solution(9508748308312653953)
XLA Ops:
  8.2 15.0 %all-reduce.3 = (f32[32]{0:T(128)S(1)}, f32[32]{0:T(128)S(1)}) all-reduce(f32[32]{0:T(128)S(1)} %get-tuple-element.9, f32[32]{0:T(128)S(1)} %get-tuple-element.8), channel_id=1, replica_groups=mesh['dp'=32,'tensor'=8] {'tensor'}, use_global_device_ids=true, to_apply=%region_3.0 | all-reduce | flops 64 | bytes 512 | tf_op jit(solution)/shard_map/psum | solution.py:43
  23.3 1.5 fusion.8
  24.9 74.0 %all-gather.4.cloned.1.call-done = bf16[1024,768]{1,0:T(8,128)(2,1)} async-done(((bf16[32,768]{1,0:T(8,128)(2,1)}), bf16[1024,768]{1,0:T(8,128)(2,1)}) %all-gather.4.cloned.1.call-update) | async-done | bytes 1572880 | tf_op jit(solution)/shard_map/all_gather | solution.py:48
  98.8 4.9 fusion.14
  103.7 4.4 fusion.12
  108.1 91.1 %all-reduce.7.cloned.1.call-done = (f32[1024,768]{1,0:T(8,128)}, f32[1024,768]{1,0:T(8,128)}) async-done(((f32[1024,768]{1,0:T(8,128)}, f32[1024,768]{1,0:T(8,128)}), (f32[1024,768]{1,0:T(8,128)}, f32[1024,768]{1,0:T(8,128)})) %all-reduce.7.cloned.1.call-update) | async-done | bytes 6291472 | tf_op jit(solution)/shard_map/psum | solution.py:52
  199.2 3.0 multiply_convert_fusion.1
  202.2 1.4 fusion.13
  203.9 1.4 copy-done.2
  205.2 1.4 fusion.4
  206.7 1.4 convolution_add_fusion
  208.1 3.2 pad_maximum_fusion
  211.4 6.6 %copy.16 = f32[1024,1536]{1,0:T(8,128)} copy(f32[1024,1536]{0,1:T(8,128)} %pad_maximum_fusion) | data formatting | bytes 12582912
  218.7 218.9 %reduce-scatter.7.cloned.1.call-done = f32[32,1536]{1,0:T(8,128)} async-done(((f32[1024,1536]{1,0:T(8,128)}), f32[32,1536]{1,0:T(8,128)}) %reduce-scatter.7.cloned.1.call-update) | async-done | bytes 196624 | tf_op jit(solution)/shard_map/reduce_scatter | solution.py:65
  438.6 16.9 %all-reduce.2 = (f32[32]{0:T(128)S(1)}, f32[32]{0:T(128)S(1)}) all-reduce(f32[32]{0:T(128)S(1)} %get-tuple-element.7, f32[32]{0:T(128)S(1)} %get-tuple-element.6), channel_id=1, replica_groups=mesh['dp'=32,'tensor'=8] {'tensor'}, use_global_device_ids=true, to_apply=%region_12.0 | all-reduce | flops 64 | bytes 512 | tf_op jit(solution)/shard_map/psum | solution.py:72
  456.6 12.4 %all-reduce.1 = (f32[32]{0:T(128)S(1)}, f32[32]{0:T(128)S(1)}) all-reduce(f32[32]{0:T(128)S(1)} %get-tuple-element.3, f32[32]{0:T(128)S(1)} %get-tuple-element.2), channel_id=1, replica_groups=mesh['dp'=32,'tensor'=8] {'tensor'}, use_global_device_ids=true, to_apply=%region_14.0 | all-reduce | flops 64 | bytes 512 | tf_op jit(solution)/shard_map/psum | solution.py:76
  470.1 12.4 %all-reduce = (f32[32]{0:T(128)S(1)}, f32[32]{0:T(128)S(1)}) all-reduce(f32[32]{0:T(128)S(1)} %get-tuple-element.5, f32[32]{0:T(128)S(1)} %get-tuple-element.4), channel_id=1, replica_groups=mesh['dp'=32,'tensor'=8] {'tensor'}, use_global_device_ids=true, to_apply=%region_18.0 | all-reduce | flops 64 | bytes 512 | tf_op jit(solution)/shard_map/psum | solution.py:85
  483.3 68.7 %all-gather.6.cloned.1.call-done = bf16[1024,768]{1,0:T(8,128)(2,1)} async-done(((bf16[32,768]{1,0:T(8,128)(2,1)}), bf16[1024,768]{1,0:T(8,128)(2,1)}) %all-gather.6.cloned.1.call-update) | async-done | bytes 1572880 | tf_op jit(solution)/shard_map/all_gather | solution.py:96
  552.1 4.5 fusion.15
  557.9 36.3 %reduce-scatter.5.cloned.1.call-done = f32[128,768]{1,0:T(8,128)} async-done(((f32[1024,768]{1,0:T(8,128)}), f32[128,768]{1,0:T(8,128)}) %reduce-scatter.5.cloned.1.call-update) | async-done | bytes 393232 | tf_op jit(solution)/shard_map/reduce_scatter | solution.py:103
  594.1 1.7 multiply_convert_fusion.3
  595.9 4.3 fusion.17
  600.1 25.4 %all-gather.8.cloned.1.call-done = bf16[1024,768]{1,0:T(8,128)(2,1)} async-done(((bf16[128,768]{1,0:T(8,128)(2,1)}), bf16[1024,768]{1,0:T(8,128)(2,1)}) %all-gather.8.cloned.1.call-update) | async-done | bytes 1572880 | tf_op jit(solution)/shard_map/all_gather | solution.py:105
  625.5 4.7 fusion.16
  (41 shorter events, 7.4 us)
Async XLA Ops:
  7.2 195.0 %copy-start = (bf16[768,768]{1,0:T(8,128)(2,1)S(1)}, bf16[768,768]{1,0:T(8,128)(2,1)}, u32[]{:S(2)}) copy-start(bf16[768,768]{1,0:T(8,128)(2,1)} %param.15) | copy-start | bytes 3538948
  7.2 91.7 %all-gather.4.cloned.1.call-start = ((), (), s32[]{:S(2)}) async-start(), calls=%async_computation.2 | async-start | bytes 1622016 | tf_op jit(solution)/shard_map/all_gather | solution.py:48
  24.8 174.4 %all-reduce.7.cloned.1.call-start = ((), (), s32[]{:S(2)}) async-start(), calls=%async_computation.7 | async-start | bytes 12582912 | tf_op jit(solution)/shard_map/psum | solution.py:52
  98.8 4.9 copy-start.8
  108.1 91.1 %copy-start.7 = (f32[768]{0:T(1024)S(1)}, f32[768]{0:T(1024)}, u32[]{:S(2)}) copy-start(f32[768]{0:T(1024)} %param.14) | copy-start | bytes 9220
  108.1 329.5 %reduce-scatter.7.cloned.1.call-start = ((), (), s32[]{:S(2)}) async-start(), calls=%async_computation.6 | async-start | bytes 6488064 | tf_op jit(solution)/shard_map/reduce_scatter | solution.py:65
  202.2 1.7 copy-start.1
  202.2 3.0 copy-start.2
  205.2 1.4 copy-start.3
  218.0 0.7 copy-start.6
  218.0 219.6 %copy-start.4 = (bf16[32,768]{1,0:T(8,128)(2,1)S(1)}, bf16[32,768]{1,0:T(8,128)(2,1)}, u32[]{:S(2)}) copy-start(bf16[32,768]{1,0:T(8,128)(2,1)} %param.10) | copy-start | bytes 147460
  218.0 251.0 %copy-start.5 = (f32[32,768]{1,0:T(8,128)S(1)}, f32[32,768]{1,0:T(8,128)}, u32[]{:S(2)}) copy-start(f32[32,768]{1,0:T(8,128)} %param.17) | copy-start | bytes 294916
  218.0 334.1 %all-gather.6.cloned.1.call-start = ((), (), s32[]{:S(2)}) async-start(), calls=%async_computation.3 | async-start | bytes 1622016 | tf_op jit(solution)/shard_map/all_gather | solution.py:96
  483.3 110.8 %reduce-scatter.5.cloned.1.call-start = ((), (), s32[]{:S(2)}) async-start(), calls=%async_computation.4 | async-start | bytes 3538944 | tf_op jit(solution)/shard_map/reduce_scatter | solution.py:103
  556.6 68.9 %all-gather.8.cloned.1.call-start = ((), (), s32[]{:S(2)}) async-start(), calls=%async_computation.5 | async-start | bytes 1769472 | tf_op jit(solution)/shard_map/all_gather | solution.py:105
Sparse Core Ops, SparseCore 0:
  24.9 73.8 all-gather.3
  108.2 90.9 all-reduce.6
  218.1 219.3 reduce-scatter.6
  483.4 68.6 all-gather.5
  556.7 37.3 reduce-scatter.4
  596.5 28.8 all-gather.7
where the time goes:
time: 638 us; the launch traced here: 637 us
  waiting for transfers between devices  514 us (81%)
  blocking collectives  56.8 us (9%)
  matrix products  27 us (4%)
  other arithmetic  14.4 us (2%)
  between operations  14.2 us (2%)
  local copies, waits for them, and re-layouts  9.84 us (2%)
    reduce_scatter x1, waiting for transfers between devices, on_device(): lax.psum_scatter(jnp.concatenate([primal, tangent], axis=1), 'dp', scatte...  219 us
    psum x1, waiting for transfers between devices, on_device(): pre_total, tangent_total = lax.psum((pre_part, tangent_part), 'tensor')  91.1 us
    all_gather x1, waiting for transfers between devices, on_device(): all_normed = lax.all_gather(normed, 'dp', axis=0, tiled=True)  74 us
    all_gather x1, waiting for transfers between devices, on_device(): all_cotangent = lax.all_gather(cotangent, 'dp', axis=0, tiled=True)  68.7 us
    reduce_scatter x1, waiting for transfers between devices, on_device(): lax.psum_scatter(back_part, 'tensor', scatter_dimension=0, tiled=True)  36.3 us
    all_gather x1, waiting for transfers between devices, on_device(): grad_pre = lax.all_gather(grad_share, 'tensor', axis=0, tiled=True)  25.4 us
    psum x1, blocking collectives, on_device(): lax.psum((row_total(output), row_total(output * output)), 'tensor')  16.9 us
    psum x1, blocking collectives, on_device(): lax.psum((row_total(source), row_total(source * source)), 'tensor')  15 us
  transfers between devices with their start and end apart: 6, of which 6 were waited for; matrix products, arithmetic and copies ran while one was open for 1% of the time, Pallas kernels for 0%

commit v1 on v0

v1 whole, which is shorter than its diff:
```python
import functools

import jax
import jax.numpy as jnp
from jax import lax
from jax.experimental import pallas as pl
from jax.experimental.pallas import tpu as pltpu
from jax.sharding import PartitionSpec as P

D = 6144
epsilon = 1e-05
root_half = 0.7071067811865476
inv_root_two_pi = 0.3989422804014327

f32 = jnp.float32
bf16 = jnp.bfloat16
MESH = pl.DeviceIdType.MESH

NX, NZ, NY = 4, 8, 4
OWN = 16
QUARTER = NZ * OWN
SHARE = QUARTER // NY
ROWS = NX * QUARTER
W = 768
TILE = 256
TILES = W // TILE
X_OFFSETS = (0, 1, 3, 2)
Z_NEAR = (1, 7, 2, 6, 3, 5, 4)
Z_FAR = (4, 3, 5, 2, 6, 1, 7)
Y_ORDER = (2, 1, 3)

N_SEND = 160
N_RECV = 120
N_LOCAL = 24


def dot(a, b):
    return jnp.dot(a, b, preferred_element_type=f32)


def dot_last(a, b):
    return lax.dot_general(a, b, (((1,), (1,)), ((), ())), preferred_element_type=f32)


def dot_first(a, b):
    return lax.dot_general(a, b, (((0,), (0,)), ((), ())), preferred_element_type=f32)


def columns(values):
    lane = lax.broadcasted_iota(jnp.int32, (OWN, 128), 1)
    out = jnp.zeros((OWN, 128), f32)
    for at, value in enumerate(values):
        out = jnp.where(lane == at, value, out)
    return out


def row_sum(pair):
    return jnp.sum(pair[0] + pair[1], axis=1, keepdims=True)


def kernel(
    tokens, gain_in, shift_in, up_weight, up_bias, down_weight, gain_out, curvature, up_tangent, down_tangent,
    up_out, down_out,
    w_up, w_ut, w_dn, w_dt, tok, curv, gin_x, sin_x, gout_x,
    stat_a, stat_b, normed, normed_x, part_f, part_s, part_r, part_own,
    both, hidden_x, slope, own_x, out_s, out_r, sum_s, sum_r,
    cot, cot_x, back_f, back_s, back_r, back_own, grad, grad_x, stage,
    send_sem, recv_sem, local_sem,
):
    d, t = lax.axis_index("dp"), lax.axis_index("tensor")
    x, z = d // NZ, lax.rem(d, NZ)
    y, c = t // 2, lax.rem(t, 2)
    other = 1 - c

    def at_x(k):
        return (lax.rem(x + k, NX) * NZ + z, t)

    def at_z(k):
        return (x * NZ + lax.rem(z + k, NZ), t)

    def at_y(k):
        return (d, lax.rem(y + k, NY) * 2 + c)

    sibling = (d, y * 2 + other)
    sends, locals_, counts = [], [], {"send": 0, "recv": 0, "local": 0}

    def fresh(kind, n=1):
        at = counts[kind]
        counts[kind] += n
        return at

    def copy_to(src, dst, device, slot):
        copy = pltpu.make_async_remote_copy(
            src_ref=src, dst_ref=dst, send_sem=send_sem.at[fresh("send")],
            recv_sem=recv_sem.at[slot], device_id=device, device_id_type=MESH,
        )
        copy.start()
        sends.append(copy)

    def arrived(dst, slot):
        pltpu.make_async_remote_copy(
            src_ref=dst, dst_ref=dst, send_sem=send_sem.at[0],
            recv_sem=recv_sem.at[slot], device_id=sibling, device_id_type=MESH,
        ).wait_recv()

    def copy_here(src, dst):
        copy = pltpu.make_async_copy(src, dst, local_sem.at[fresh("local")])
        copy.start()
        return copy

    own_rows = pl.ds(pl.multiple_of(c * OWN, OWN), OWN)
    their_rows = pl.ds(pl.multiple_of(other * OWN, OWN), OWN)
    tok_here = copy_here(tokens.at[own_rows], tok.at[c])
    curv_here = copy_here(curvature.at[own_rows], curv.at[c])
    up_here = [copy_here(up_weight, w_up.at[c]), copy_here(up_tangent, w_ut.at[c])]
    down_here = [copy_here(down_weight, w_dn.at[c]), copy_here(down_tangent, w_dt.at[c])]
    barrier = pltpu.get_barrier_semaphore()
    peers = [sibling] + [at_x(k) for k in range(1, NX)] + [at_z(k) for k in range(1, NZ)] + [at_y(k) for k in range(1, NY)]
    for peer in peers:
        pl.semaphore_signal(barrier, inc=1, device_id=peer, device_id_type=MESH)
    pl.semaphore_wait(barrier, len(peers))

    tok_slot, params_slot, curv_slot = fresh("recv"), fresh("recv", 3), fresh("recv")
    up_slot, down_slot = fresh("recv", 2), fresh("recv", 2)
    copy_to(tokens.at[their_rows], tok.at[c], sibling, tok_slot)
    copy_to(gain_in, gin_x, sibling, params_slot)
    copy_to(shift_in, sin_x, sibling, params_slot + 1)
    copy_to(gain_out, gout_x, sibling, params_slot + 2)
    copy_to(up_weight, w_up.at[c], sibling, up_slot)
    copy_to(up_tangent, w_ut.at[c], sibling, up_slot + 1)
    copy_to(curvature.at[their_rows], curv.at[c], sibling, curv_slot)
    copy_to(down_weight, w_dn.at[c], sibling, down_slot)
    copy_to(down_tangent, w_dt.at[c], sibling, down_slot + 1)

    tok_here.wait()
    arrived(tok.at[other], tok_slot)
    source = tok[...].astype(f32)
    total = row_sum(source)
    spread = source - (total / (2 * W))[None]
    stat_a[0] = columns([total, row_sum(spread * spread)])
    stat_slot = fresh("recv", 3)
    for k in Y_ORDER:
        copy_to(stat_a.at[0], stat_a.at[k], at_y(k), stat_slot + k - 1)
    arrived(gin_x, params_slot)
    arrived(sin_x, params_slot + 1)
    arrived(gout_x, params_slot + 2)

    def by_half(mine, theirs):
        mine, theirs = mine[...].reshape(1, W), theirs[...].reshape(1, W)
        first = jnp.where(c == 0, mine, theirs)
        second = jnp.where(c == 0, theirs, mine)
        return jnp.stack([first, second])

    gain, shift = by_half(gain_in, gin_x), by_half(shift_in, sin_x)
    for k in range(1, NY):
        arrived(stat_a.at[k], stat_slot + k - 1)
    totals = [stat_a[k][:, 0:1] for k in range(NY)]
    center = (totals[0] + totals[1] + totals[2] + totals[3]) / D
    variance = jnp.zeros_like(center)
    for k in range(NY):
        off = totals[k] / (2 * W) - center
        variance = variance + stat_a[k][:, 1:2] + (2 * W) * (off * off)
    inverse = lax.rsqrt(variance / D + epsilon)
    block = pl.ds(pl.multiple_of(x * QUARTER + z * OWN, OWN), OWN)
    normed[:, block] = ((source - center[None]) * inverse[None] * gain + shift).astype(bf16)

    def rows_of(k):
        return pl.multiple_of(lax.rem(x + X_OFFSETS[k], NX) * QUARTER, QUARTER)

    def gather_start(array):
        z_slot, x_slot = fresh("recv", NZ), fresh("recv", NX)
        for k in Z_FAR:
            copy_to(array.at[:, block], array.at[:, block], at_z(k), z_slot + k)
        for k in (2, 1, 3):
            copy_to(array.at[:, block], array.at[:, block], at_x(k), x_slot + k)
        for k in Z_NEAR:
            from_z = lax.rem(z + NZ - k, NZ)
            landed = pl.ds(pl.multiple_of(x * QUARTER + from_z * OWN, OWN), OWN)
            arrived(array.at[:, landed], z_slot + k)
            for j in (2, 1, 3):
                copy_to(array.at[:, landed], array.at[:, landed], at_x(j), x_slot + j)
        return x_slot

    def gather_wait(array, x_slot, k):
        if k > 0:
            step = (NX - X_OFFSETS[k]) % NX
            arrived(array.at[:, pl.ds(rows_of(k), QUARTER)], x_slot + step)

    normed_slot = gather_start(normed)

    share_slot = fresh("recv", 12)
    both_slot = fresh("recv", 12)
    normed_x_slot, hidden_x_slot = fresh("recv", 4), fresh("recv", 4)
    cot_x_slot, grad_x_slot = fresh("recv", 4), fresh("recv", 4)
    out_slot = fresh("recv", NX)

    def up_step(k):
        gather_wait(normed, normed_slot, k)
        at = rows_of(k)
        rows = pl.ds(at, QUARTER)
        copy_to(normed.at[other, rows], normed_x.at[rows], sibling, normed_x_slot + k)
        if k == 0:
            for copy in up_here:
                copy.wait()
            arrived(w_up.at[other], up_slot)
            arrived(w_ut.at[other], up_slot + 1)
        left, right = normed[0, rows], normed[1, rows]

        @pl.loop(0, TILES)
        def _(n):
            cols = pl.ds(pl.multiple_of(n * TILE, TILE), TILE)
            part_f[0, :, cols] = dot(left, w_up[0, :, cols]) + dot(right, w_up[1, :, cols])
            part_f[1, :, cols] = dot(left, w_ut[0, :, cols]) + dot(right, w_ut[1, :, cols])

        for j in Y_ORDER:
            theirs = pl.ds(pl.multiple_of(lax.rem(y + j, NY) * SHARE, SHARE), SHARE)
            part_s[k, j - 1] = part_f[:, theirs].astype(bf16)
            copy_to(part_s.at[k, j - 1], part_r.at[k, j - 1], at_y(j), share_slot + k * 3 + j - 1)
        part_own[k] = part_f[:, pl.ds(pl.multiple_of(y * SHARE, SHARE), SHARE)]

    def share_rows(k, who):
        return pl.ds(pl.multiple_of(rows_of(k) + who * SHARE, SHARE), SHARE)

    def act_step(k):
        sums = part_own[k]
        for j in range(1, NY):
            arrived(part_r.at[k, j - 1], share_slot + k * 3 + j - 1)
            sums = sums + part_r[k, j - 1].astype(f32)
        pre = sums[0] + up_bias[...].reshape(1, W)
        phi = 0.5 * (1.0 + lax.erf(pre * root_half))
        derivative = phi + pre * jnp.exp(-0.5 * pre * pre) * inv_root_two_pi
        rows = share_rows(k, y)
        both[0, rows] = (pre * phi).astype(bf16)
        both[1, rows] = (derivative * sums[1]).astype(bf16)
        slope[k] = derivative.astype(bf16)
        for j in Y_ORDER:
            copy_to(both.at[:, rows], both.at[:, rows], at_y(j), both_slot + k * 3 + j - 1)

    def down_step(k):
        for j in range(1, NY):
            arrived(both.at[:, share_rows(k, lax.rem(y + NY - j, NY))], both_slot + k * 3 + j - 1)
        rows = pl.ds(rows_of(k), QUARTER)
        copy_to(both.at[0, rows], hidden_x.at[rows], sibling, hidden_x_slot + k)
        if k == 0:
            for copy in down_here:
                copy.wait()
            arrived(w_dn.at[other], down_slot)
            arrived(w_dt.at[other], down_slot + 1)
        hidden, hidden_tangent = both[0, rows], both[1, rows]

        @pl.loop(0, TILES)
        def _(n):
            cols = pl.ds(pl.multiple_of(n * TILE, TILE), TILE)
            for f in range(2):
                weight = w_dn[f, :, cols]
                primal = dot(hidden, weight)
                tangent = dot(hidden_tangent, weight) + dot(hidden, w_dt[f, :, cols])
                if k == 0:
                    own_x[0, f, :, cols] = primal
                    own_x[1, f, :, cols] = tangent
                else:
                    out_s[k - 1, 0, f, :, cols] = primal.astype(bf16)
                    out_s[k - 1, 1, f, :, cols] = tangent.astype(bf16)

        if k > 0:
            step = X_OFFSETS[k]
            copy_to(out_s.at[k - 1], out_r.at[step - 1], at_x(step), out_slot + step)

    up_step(0)
    up_step(1)
    up_step(2)
    act_step(0)
    up_step(3)
    act_step(1)
    down_step(0)
    act_step(2)
    down_step(1)
    act_step(3)
    down_step(2)
    down_step(3)

    for step in range(1, NX):
        arrived(out_r.at[step - 1], out_slot + step)

    def summed(who):
        rows = pl.ds(pl.multiple_of(who * OWN, OWN), OWN)
        value = own_x[:, :, rows]
        for step in range(1, NX):
            value = value + out_r[step - 1, :, :, rows].astype(f32)
        return value

    sum_slot = fresh("recv", NZ)
    for k in Z_FAR:
        sum_s[k - 1] = summed(lax.rem(z + k, NZ)).astype(bf16)
        copy_to(sum_s.at[k - 1], sum_r.at[k - 1], at_z(k), sum_slot + k)
    outputs = summed(z)
    arrived(curv.at[other], curv_slot)
    curv_here.wait()
    gain = by_half(gain_out, gout_x)
    factor = gain * gain * curv[...]
    for k in Z_NEAR:
        arrived(sum_r.at[k - 1], sum_slot + k)
        outputs = outputs + sum_r[k - 1].astype(f32)

    output = tok[...].astype(f32) + outputs[0]
    tangent = outputs[1]
    total = row_sum(output)
    around = output - (total / (2 * W))[None]
    factor_around = factor * around
    stat_b[0] = columns([
        total, row_sum(around * around), row_sum(tangent), row_sum(around * tangent),
        row_sum(factor), row_sum(factor_around), row_sum(factor_around * around),
        row_sum(factor * tangent), row_sum(factor_around * tangent),
    ])
    stat_slot = fresh("recv", 3)
    for k in Y_ORDER:
        copy_to(stat_b.at[0], stat_b.at[k], at_y(k), stat_slot + k - 1)
    for k in range(1, NY):
        arrived(stat_b.at[k], stat_slot + k - 1)
    stats = [[stat_b[k][:, i:i + 1] for i in range(9)] for k in range(NY)]
    center = (stats[0][0] + stats[1][0] + stats[2][0] + stats[3][0]) / D
    zero = jnp.zeros_like(center)
    square, sum_t, dot_t, f_0, f_1, f_2, ft_0, ft_1 = (zero,) * 8
    for s in stats:
        off = s[0] / (2 * W) - center
        square = square + s[1] + (2 * W) * (off * off)
        sum_t = sum_t + s[2]
        dot_t = dot_t + s[3] + off * s[2]
        f_0 = f_0 + s[4]
        f_1 = f_1 + s[5] + off * s[4]
        f_2 = f_2 + s[6] + 2.0 * off * s[5] + off * off * s[4]
        ft_0 = ft_0 + s[7]
        ft_1 = ft_1 + s[8] + off * s[7]
    inverse = lax.rsqrt(square / D + epsilon)
    mean_t = sum_t / D
    mean_nt = dot_t * inverse / D
    fn_1 = f_1 * inverse
    mean_w = (ft_0 - mean_t * f_0 - mean_nt * fn_1) * inverse / D
    mean_nw = (ft_1 * inverse - mean_t * fn_1 - mean_nt * (f_2 * inverse * inverse)) * inverse / D
    normal = (output - center[None]) * inverse[None]
    weighted = factor * ((tangent - mean_t[None] - normal * mean_nt[None]) * inverse[None])
    cot[:, block] = ((weighted - mean_w[None] - normal * mean_nw[None]) * inverse[None]).astype(bf16)

    cot_slot = gather_start(cot)
    back_slot = fresh("recv", 12)
    grad_slot = fresh("recv", 12)

    def back_step(k):
        gather_wait(cot, cot_slot, k)
        rows = pl.ds(rows_of(k), QUARTER)
        copy_to(cot.at[other, rows], cot_x.at[rows], sibling, cot_x_slot + k)
        left, right = cot[0, rows], cot[1, rows]

        @pl.loop(0, TILES)
        def _(n):
            units = pl.ds(pl.multiple_of(n * TILE, TILE), TILE)
            back_f[:, units] = dot_last(left, w_dn[0, units]) + dot_last(right, w_dn[1, units])

        for j in Y_ORDER:
            theirs = pl.ds(pl.multiple_of(lax.rem(y + j, NY) * SHARE, SHARE), SHARE)
            back_s[k, j - 1] = back_f[theirs].astype(bf16)
            copy_to(back_s.at[k, j - 1], back_r.at[k, j - 1], at_y(j), back_slot + k * 3 + j - 1)
        back_own[k] = back_f[pl.ds(pl.multiple_of(y * SHARE, SHARE), SHARE)]

    def grad_step(k):
        sums = back_own[k]
        for j in range(1, NY):
            arrived(back_r.at[k, j - 1], back_slot + k * 3 + j - 1)
            sums = sums + back_r[k, j - 1].astype(f32)
        rows = share_rows(k, y)
        grad[rows] = (sums * slope[k].astype(f32)).astype(bf16)
        for j in Y_ORDER:
            copy_to(grad.at[rows], grad.at[rows], at_y(j), grad_slot + k * 3 + j - 1)

    def swap_step(k):
        for j in range(1, NY):
            arrived(grad.at[share_rows(k, lax.rem(y + NY - j, NY))], grad_slot + k * 3 + j - 1)
        rows = pl.ds(rows_of(k), QUARTER)
        copy_to(grad.at[rows], grad_x.at[rows], sibling, grad_x_slot + k)

    def product(first, first_x, second, second_x, result, slot):
        copies = []
        for n in range(TILES):
            part = pl.ds(n * TILE, TILE)
            stage[slot, part] = dot_first(first(part), second[...]) + dot_first(first_x(part), second_x[...])
            copies.append(copy_here(stage.at[slot, part], result.at[part]))
        return copies

    back_step(0)
    back_step(1)
    back_step(2)
    grad_step(0)
    back_step(3)
    grad_step(1)
    grad_step(2)
    grad_step(3)
    everything = pl.ds(0, ROWS)
    for k in range(NX):
        theirs = pl.ds(rows_of(k), QUARTER)
        arrived(hidden_x.at[theirs], hidden_x_slot + k)
        arrived(cot_x.at[theirs], cot_x_slot + k)
        arrived(normed_x.at[theirs], normed_x_slot + k)
    written = product(
        lambda part: both[0, :, part], lambda part: hidden_x[:, part], cot.at[c], cot_x, down_out, 0,
    )
    for k in range(NX):
        swap_step(k)
    for k in range(NX):
        arrived(grad_x.at[pl.ds(rows_of(k), QUARTER)], grad_x_slot + k)
    written += product(
        lambda part: normed[c, :, part], lambda part: normed_x[:, part], grad, grad_x, up_out, 1,
    )
    for copy in written:
        copy.wait()
    for copy in sends:
        copy.wait_send()


def on_device(*args):
    any_ = pl.BlockSpec(memory_space=pl.ANY)
    vmem = pl.BlockSpec(memory_space=pltpu.VMEM)
    scratch = [
        ((2, W, W), bf16), ((2, W, W), bf16), ((2, W, W), bf16), ((2, W, W), bf16),
        ((2, OWN, W), bf16), ((2, OWN, W), f32), ((W,), f32), ((W,), f32), ((W,), f32),
        ((NY, OWN, 128), f32), ((NY, OWN, 128), f32),
        ((2, ROWS, W), bf16), ((ROWS, W), bf16),
        ((2, QUARTER, W), f32), ((NX, 3, 2, SHARE, W), bf16), ((NX, 3, 2, SHARE, W), bf16), ((NX, 2, SHARE, W), f32),
        ((2, ROWS, W), bf16), ((ROWS, W), bf16), ((NX, SHARE, W), bf16),
        ((2, 2, QUARTER, W), f32), ((3, 2, 2, QUARTER, W), bf16), ((3, 2, 2, QUARTER, W), bf16),
        ((NZ - 1, 2, 2, OWN, W), bf16), ((NZ - 1, 2, 2, OWN, W), bf16),
        ((2, ROWS, W), bf16), ((ROWS, W), bf16),
        ((QUARTER, W), f32), ((NX, 3, SHARE, W), bf16), ((NX, 3, SHARE, W), bf16), ((NX, SHARE, W), f32),
        ((ROWS, W), bf16), ((ROWS, W), bf16), ((2, W, W), f32),
    ]
    return pl.pallas_call(
        kernel,
        out_shape=(jax.ShapeDtypeStruct((W, W), f32), jax.ShapeDtypeStruct((W, W), f32)),
        in_specs=[any_, vmem, vmem, any_, vmem, any_, vmem, any_, any_, any_],
        out_specs=(any_, any_),
        scratch_shapes=[pltpu.VMEM(shape, dtype) for shape, dtype in scratch]
        + [pltpu.SemaphoreType.DMA((N_SEND,)), pltpu.SemaphoreType.DMA((N_RECV,)), pltpu.SemaphoreType.DMA((N_LOCAL,))],
        compiler_params=pltpu.CompilerParams(
            collective_id=0, has_side_effects=True, vmem_limit_bytes=60 * 2**20
        ),
        cost_estimate=pl.CostEstimate(flops=9663676416, bytes_accessed=9437184, transcendentals=262144),
        name="gauss_newton",
    )(*args)


def solution(mesh):
    return jax.shard_map(
        on_device,
        mesh=mesh,
        in_specs=(
            P("dp", "tensor"),
            P("tensor"),
            P("tensor"),
            P("tensor", "dp"),
            P("dp"),
            P("dp", "tensor"),
            P("tensor"),
            P("dp", "tensor"),
            P("tensor", "dp"),
            P("dp", "tensor"),
        ),
        out_specs=(P("tensor", "dp"), P("dp", "tensor")),
        check_vma=False,
    )
```

time: 638 us -> 182 us (0.29)
  waiting for transfers between devices: 514 us -> 0 us
  Pallas kernels: 0 us -> 177 us
  blocking collectives: 56.8 us -> 0 us
  matrix products: 27 us -> 0 us
  other arithmetic: 14.4 us -> 0 us
  between operations: 14.2 us -> 0.65 us
    reduce_scatter x2 -> x0, waiting for transfers between devices: 255 us -> none  [the longest x1 219 us: on_device(): lax.psum_scatter(jnp.concatenate([primal, tangent], axis=1), 'dp', scatte...]
    pallas_call x0 -> x1, Pallas kernels: none -> 177 us  [on_device(): pl.pallas_call(kernel, out_shape=(jax.ShapeDtypeStruct((W, W), f32), jax....]
    all_gather x3 -> x0, waiting for transfers between devices: 168 us -> none  [the longest x1 74 us: on_device(): all_normed = lax.all_gather(normed, 'dp', axis=0, tiled=True)]
    psum x1 -> x0, waiting for transfers between devices: 91.1 us -> none  [on_device(): pre_total, tangent_total = lax.psum((pre_part, tangent_part), 'tensor')]
    psum x4 -> x0, blocking collectives: 56.8 us -> none  [the longest x1 16.9 us: on_device(): lax.psum((row_total(output), row_total(output * output)), 'tensor')]
    dot_general x8 -> x0, matrix products: 27 us -> none  [the longest x1 4.88 us: on_device(): jnp.dot(all_normed, up_tangent, preferred_element_type=jnp.float32)]
    convert_element_type x4 -> x0, other arithmetic: 6.92 us -> none  [the longest x1 2.97 us: on_device(): hidden = gelu_value(pre_full).astype(jnp.bfloat16)]
  transfers between devices with their start and end apart: 6 -> 0, of which waited for: 6 -> 0; matrix products, arithmetic and copies ran while one was open for 1% -> 0% of each run, Pallas kernels for 0% -> 0%
where the time goes in v1:
time: 182 us
  Pallas kernels  177 us (97%)
  local copies, waits for them, and re-layouts  4.78 us (3%)
    pallas_call x1, Pallas kernels, on_device(): pl.pallas_call(kernel, out_shape=(jax.ShapeDtypeStruct((W, W), f32), jax....  177 us
    unnamed x4, local copies, waits for them, and re-layouts  4.78 us

profile of v1, /device:TPU:1, one launch (start us, length us, event | category | flops | bytes accessed | tf_op | source)
XLA Modules:
  0.0 182.2 jit_solution(11845992374778024556)
XLA Ops:
  0.6 176.8 %gauss_newton.1 = (f32[768,768]{1,0:T(8,128)}, f32[768,768]{1,0:T(8,128)}) custom-call(bf16[32,768]{1,0:T(8,128)(2,1)} %tokens.1, f32[768]{0:T(1024)} %gain_in.1, f32[768]{0:T(1024)} %shift_in.1, bf16[768,768]{1,0:T(8,128)(2,1)} %up_weight.1, f32[768]{0:T(1024)} %up_bias.1, bf16[768,768]{1,0:T(8,128)(2,1)} %down_weight.1, f32[768]{0:T(1024)} %gain_out.1, ...), custom_call_target="tpu_custom_call" | custom-call | flops 9663676416 | bytes 9437184 | tf_op jit(solution)/shard_map/gauss_newton/pallas_call | solution.py:435
  177.4 0.0 copy-start
  177.4 3.4 %copy.14 = f32[768,768]{1,0:T(8,128)} copy(f32[768,768]{1,0:T(8,128)} %get-tuple-element.4) | data formatting | bytes 4718592
  180.8 0.0 copy-done
  180.8 1.4 copy.15
Async XLA Ops:
  177.4 3.4 %copy-start = (f32[768,768]{1,0:T(8,128)S(1)}, f32[768,768]{1,0:T(8,128)}, u32[]{:S(2)}) copy-start(f32[768,768]{1,0:T(8,128)} %get-tuple-element.5) | copy-start | bytes 7077892

commit v2 on v1

v2 whole, which is shorter than its diff:
```python
import functools

import jax
import jax.numpy as jnp
from jax import lax
from jax.experimental import pallas as pl
from jax.experimental.pallas import tpu as pltpu
from jax.sharding import PartitionSpec as P

D = 6144
epsilon = 1e-05
root_half = 0.7071067811865476
inv_root_two_pi = 0.3989422804014327

f32 = jnp.float32
bf16 = jnp.bfloat16
MESH = pl.DeviceIdType.MESH

NX, NZ, NY = 4, 8, 4
OWN = 16
GROUP = NX * OWN
ROWS = NZ * GROUP
W = 768
TILE = 256
TILES = W // TILE
FORWARD = ((1, 7), (4,), (3, 5), (2, 6), (0,))
BACKWARD = ((0,), (1, 7), (2, 6), (3, 5), (4,))
NEAR = (1, 7)
FAR = (4, 3, 5, 2, 6)
J_ORDER = (2, 1, 3)

N_SEND = 320
N_RECV = 400
N_LOCAL = 24


def dot(a, b):
    return jnp.dot(a, b, preferred_element_type=f32)


def dot_last(a, b):
    return lax.dot_general(a, b, (((1,), (1,)), ((), ())), preferred_element_type=f32)


def dot_first(a, b):
    return lax.dot_general(a, b, (((0,), (0,)), ((), ())), preferred_element_type=f32)


def columns(values):
    lane = lax.broadcasted_iota(jnp.int32, (OWN, 128), 1)
    out = jnp.zeros((OWN, 128), f32)
    for at, value in enumerate(values):
        out = jnp.where(lane == at, value, out)
    return out


def row_sum(pair):
    return jnp.sum(pair[0] + pair[1], axis=1, keepdims=True)


def kernel(
    tokens, gain_in, shift_in, up_weight, up_bias, down_weight, gain_out, curvature, up_tangent, down_tangent,
    up_out, down_out,
    w_up, w_ut, w_dn, w_dt, tok, curv, gin_x, sin_x, gout_x,
    stat_a, stat_b, normed, normed_x, part_f, part_s, part_r, part_own,
    both, hidden_x, slope, out_f, raw_s, raw_r, own_x, out_s, out_r, sum_s, sum_r,
    cot, cot_x, back_f, back_s, back_r, back_own, grad, grad_x, stage,
    send_sem, recv_sem, local_sem,
):
    d, t = lax.axis_index("dp"), lax.axis_index("tensor")
    x, z = d // NZ, lax.rem(d, NZ)
    y, c = t // 2, lax.rem(t, 2)
    other = 1 - c

    def at_x(k):
        return (lax.rem(x + k, NX) * NZ + z, t)

    def at_z(k):
        return (x * NZ + lax.rem(z + k, NZ), t)

    def at_y(k):
        return (d, lax.rem(y + k, NY) * 2 + c)

    sibling = (d, y * 2 + other)
    sends, locals_, counts = [], [], {"send": 0, "recv": 0, "local": 0}

    def fresh(kind, n=1):
        at = counts[kind]
        counts[kind] += n
        return at

    def copy_to(src, dst, device, slot):
        copy = pltpu.make_async_remote_copy(
            src_ref=src, dst_ref=dst, send_sem=send_sem.at[fresh("send")],
            recv_sem=recv_sem.at[slot], device_id=device, device_id_type=MESH,
        )
        copy.start()
        sends.append(copy)

    def arrived(dst, slot):
        pltpu.make_async_remote_copy(
            src_ref=dst, dst_ref=dst, send_sem=send_sem.at[0],
            recv_sem=recv_sem.at[slot], device_id=sibling, device_id_type=MESH,
        ).wait_recv()

    def copy_here(src, dst):
        copy = pltpu.make_async_copy(src, dst, local_sem.at[fresh("local")])
        copy.start()
        return copy

    own_rows = pl.ds(pl.multiple_of(c * OWN, OWN), OWN)
    their_rows = pl.ds(pl.multiple_of(other * OWN, OWN), OWN)
    tok_here = copy_here(tokens.at[own_rows], tok.at[c])
    curv_here = copy_here(curvature.at[own_rows], curv.at[c])
    up_here = [copy_here(up_weight, w_up.at[c]), copy_here(up_tangent, w_ut.at[c])]
    down_here = [copy_here(down_weight, w_dn.at[c]), copy_here(down_tangent, w_dt.at[c])]
    barrier = pltpu.get_barrier_semaphore()
    peers = [sibling] + [at_x(k) for k in range(1, NX)] + [at_z(k) for k in range(1, NZ)] + [at_y(k) for k in range(1, NY)]
    for peer in peers:
        pl.semaphore_signal(barrier, inc=1, device_id=peer, device_id_type=MESH)
    pl.semaphore_wait(barrier, len(peers))

    tok_slot, params_slot, curv_slot = fresh("recv"), fresh("recv", 3), fresh("recv")
    up_slot, down_slot = fresh("recv", 2), fresh("recv", 2)
    copy_to(tokens.at[their_rows], tok.at[c], sibling, tok_slot)
    copy_to(gain_in, gin_x, sibling, params_slot)
    copy_to(shift_in, sin_x, sibling, params_slot + 1)
    copy_to(gain_out, gout_x, sibling, params_slot + 2)
    copy_to(up_weight, w_up.at[c], sibling, up_slot)
    copy_to(up_tangent, w_ut.at[c], sibling, up_slot + 1)
    copy_to(curvature.at[their_rows], curv.at[c], sibling, curv_slot)
    copy_to(down_weight, w_dn.at[c], sibling, down_slot)
    copy_to(down_tangent, w_dt.at[c], sibling, down_slot + 1)

    tok_here.wait()
    arrived(tok.at[other], tok_slot)
    source = tok[...].astype(f32)
    total = row_sum(source)
    spread = source - (total / (2 * W))[None]
    stat_a[0] = columns([total, row_sum(spread * spread)])
    stat_slot = fresh("recv", 3)
    for k in J_ORDER:
        copy_to(stat_a.at[0], stat_a.at[k], at_y(k), stat_slot + k - 1)
    arrived(gin_x, params_slot)
    arrived(sin_x, params_slot + 1)
    arrived(gout_x, params_slot + 2)

    def by_half(mine, theirs):
        mine, theirs = mine[...].reshape(1, W), theirs[...].reshape(1, W)
        first = jnp.where(c == 0, mine, theirs)
        second = jnp.where(c == 0, theirs, mine)
        return jnp.stack([first, second])

    gain, shift = by_half(gain_in, gin_x), by_half(shift_in, sin_x)
    for k in range(1, NY):
        arrived(stat_a.at[k], stat_slot + k - 1)
    totals = [stat_a[k][:, 0:1] for k in range(NY)]
    center = (totals[0] + totals[1] + totals[2] + totals[3]) / D
    variance = jnp.zeros_like(center)
    for k in range(NY):
        off = totals[k] / (2 * W) - center
        variance = variance + stat_a[k][:, 1:2] + (2 * W) * (off * off)
    inverse = lax.rsqrt(variance / D + epsilon)
    def group(k):
        return pl.ds(pl.multiple_of(lax.rem(z + NZ + k, NZ) * GROUP, GROUP), GROUP)

    def block_of(j, k):
        first = lax.rem(z + NZ + k, NZ) * GROUP + lax.rem(x + NX + j, NX) * OWN
        return pl.ds(pl.multiple_of(first, OWN), OWN)

    block = block_of(0, 0)
    normed[:, block] = ((source - center[None]) * inverse[None] * gain + shift).astype(bf16)

    def gather_start(array, far):
        def send(rows, device, slot):
            copy_to(array.at[:, rows], array.at[:, rows], device, slot)

        z_slot, x_slot = fresh("recv", NZ), fresh("recv", NX)
        near_slot, far_slot = fresh("recv", NZ * NX), fresh("recv", NZ * NX)
        for j in J_ORDER:
            send(block, at_x(j), x_slot + j)
        for k in NEAR + far:
            send(block, at_z(k), z_slot + k)
        for j in (1, 3, 2):
            rows = block_of(-j, 0)
            arrived(array.at[:, rows], x_slot + j)
            for k in NEAR:
                send(rows, at_z(k), near_slot + k * NX + j)
        for k in far:
            rows = block_of(0, -k)
            arrived(array.at[:, rows], z_slot + k)
            for j in J_ORDER:
                send(rows, at_x(j), far_slot + k * NX + j)
        return z_slot, near_slot, far_slot

    def gather_wait(array, slots, chunk):
        z_slot, near_slot, far_slot = slots
        for offset in chunk:
            k = (NZ - offset) % NZ
            if k in NEAR:
                arrived(array.at[:, block_of(0, -k)], z_slot + k)
                for j in range(1, NX):
                    arrived(array.at[:, block_of(-j, -k)], near_slot + k * NX + j)
            elif k:
                for j in range(1, NX):
                    arrived(array.at[:, block_of(-j, -k)], far_slot + k * NX + j)

    def stacked(array, chunk):
        parts = [array[group(offset)] for offset in chunk]
        return parts[0] if len(parts) == 1 else jnp.concatenate(parts, axis=0)

    normed_slots = gather_start(normed, FAR)

    share_slot = fresh("recv", 5 * NY)
    both_slot = fresh("recv", NZ * NY)
    normed_x_slot, hidden_x_slot = fresh("recv"), fresh("recv")
    cot_x_slot, grad_x_slot = fresh("recv"), fresh("recv", NZ)
    raw_slot, out_slot, sum_slot = fresh("recv", NZ), fresh("recv", NZ * NX), fresh("recv", NZ)

    def up_step(n):
        chunk = FORWARD[n]
        size = len(chunk)
        gather_wait(normed, normed_slots, chunk)
        if n == 0:
            for copy in up_here:
                copy.wait()
            arrived(w_up.at[other], up_slot)
            arrived(w_ut.at[other], up_slot + 1)
        left, right = stacked(normed.at[0], chunk), stacked(normed.at[1], chunk)
        rows = pl.ds(0, size * GROUP)
        part_f[0, rows] = dot(left, w_up[0]) + dot(right, w_up[1])
        part_f[1, rows] = dot(left, w_ut[0]) + dot(right, w_ut[1])

        def share(j):
            mine = lax.rem(y + j, NY) * OWN
            return [part_f[:, pl.ds(pl.multiple_of(i * GROUP + mine, OWN), OWN)] for i in range(size)]

        for j in J_ORDER:
            for i, value in enumerate(share(j)):
                part_s[n, j - 1, i] = value.astype(bf16)
            few = pl.ds(0, size)
            copy_to(part_s.at[n, j - 1, few], part_r.at[n, j - 1, few], at_y(j), share_slot + n * NY + j)
        for i, value in enumerate(share(0)):
            part_own[n, i] = value
        if n == len(FORWARD) - 1:
            copy_to(normed.at[other], normed_x, sibling, normed_x_slot)

    def share_rows(offset, who):
        first = lax.rem(z + offset, NZ) * GROUP + lax.rem(who + NY, NY) * OWN
        return pl.ds(pl.multiple_of(first, OWN), OWN)

    def act_step(n):
        chunk = FORWARD[n]
        few = pl.ds(0, len(chunk))
        for j in range(1, NY):
            arrived(part_r.at[n, j - 1, few], share_slot + n * NY + j)
        for i, offset in enumerate(chunk):
            sums = part_own[n, i]
            for j in range(1, NY):
                sums = sums + part_r[n, j - 1, i].astype(f32)
            pre = sums[0] + up_bias[...].reshape(1, W)
            phi = 0.5 * (1.0 + lax.erf(pre * root_half))
            derivative = phi + pre * jnp.exp(-0.5 * pre * pre) * inv_root_two_pi
            rows = share_rows(offset, y)
            both[0, rows] = (pre * phi).astype(bf16)
            both[1, rows] = (derivative * sums[1]).astype(bf16)
            slope[offset] = derivative.astype(bf16)
            for j in J_ORDER:
                copy_to(both.at[:, rows], both.at[:, rows], at_y(j), both_slot + offset * NY + j)

    def down_step(n):
        chunk = FORWARD[n]
        for offset in chunk:
            for j in range(1, NY):
                arrived(both.at[:, share_rows(offset, y - j)], both_slot + offset * NY + j)
        if n == 0:
            for copy in down_here:
                copy.wait()
            arrived(w_dn.at[other], down_slot)
            arrived(w_dt.at[other], down_slot + 1)
        if n == len(FORWARD) - 1:
            copy_to(both.at[0], hidden_x, sibling, hidden_x_slot)
        hidden, hidden_tangent = stacked(both.at[0], chunk), stacked(both.at[1], chunk)
        rows = pl.ds(0, len(chunk) * GROUP)
        for f in range(2):
            out_f[0, f, rows] = dot(hidden, w_dn[f])
            out_f[1, f, rows] = dot(hidden_tangent, w_dn[f]) + dot(hidden, w_dt[f])
        for i, offset in enumerate(chunk):
            if offset in NEAR:
                raw_s[NEAR.index(offset)] = out_f[:, :, pl.ds(i * GROUP, GROUP)].astype(bf16)
                copy_to(raw_s.at[NEAR.index(offset)], raw_r.at[NEAR.index(offset)], at_z(offset), raw_slot + offset)
                continue
            if offset == 0:
                for k in NEAR:
                    arrived(raw_r.at[NEAR.index(k)], raw_slot + k)

            def part(j):
                first = pl.multiple_of(lax.rem(x + j, NX) * OWN, OWN)
                value = out_f[:, :, pl.ds(pl.multiple_of(first + i * GROUP, OWN), OWN)]
                if offset == 0:
                    for k in range(len(NEAR)):
                        value = value + raw_r[k, :, :, pl.ds(first, OWN)].astype(f32)
                return value

            for j in J_ORDER:
                out_s[offset, j - 1] = part(j).astype(bf16)
                copy_to(out_s.at[offset, j - 1], out_r.at[offset, j - 1], at_x(j), out_slot + offset * NX + j)
            own_x[offset] = part(0)

    def summed(offset):
        value = own_x[offset]
        for j in range(1, NX):
            arrived(out_r.at[offset, j - 1], out_slot + offset * NX + j)
            value = value + out_r[offset, j - 1].astype(f32)
        return value

    def sum_step(n):
        for offset in FORWARD[n]:
            sum_s[offset] = summed(offset).astype(bf16)
            copy_to(sum_s.at[offset], sum_r.at[offset], at_z(offset), sum_slot + offset)

    up_step(0)
    up_step(1)
    act_step(0)
    up_step(2)
    act_step(1)
    down_step(0)
    up_step(3)
    act_step(2)
    down_step(1)
    up_step(4)
    act_step(3)
    down_step(2)
    sum_step(1)
    act_step(4)
    down_step(3)
    sum_step(2)
    down_step(4)
    sum_step(3)

    arrived(curv.at[other], curv_slot)
    curv_here.wait()
    gain = by_half(gain_out, gout_x)
    factor = gain * gain * curv[...]
    outputs = summed(0)
    for k in FAR:
        arrived(sum_r.at[k], sum_slot + k)
        outputs = outputs + sum_r[k].astype(f32)

    output = tok[...].astype(f32) + outputs[0]
    tangent = outputs[1]
    total = row_sum(output)
    around = output - (total / (2 * W))[None]
    factor_around = factor * around
    stat_b[0] = columns([
        total, row_sum(around * around), row_sum(tangent), row_sum(around * tangent),
        row_sum(factor), row_sum(factor_around), row_sum(factor_around * around),
        row_sum(factor * tangent), row_sum(factor_around * tangent),
    ])
    stat_slot = fresh("recv", 3)
    for k in J_ORDER:
        copy_to(stat_b.at[0], stat_b.at[k], at_y(k), stat_slot + k - 1)
    for k in range(1, NY):
        arrived(stat_b.at[k], stat_slot + k - 1)
    stats = [[stat_b[k][:, i:i + 1] for i in range(9)] for k in range(NY)]
    center = (stats[0][0] + stats[1][0] + stats[2][0] + stats[3][0]) / D
    zero = jnp.zeros_like(center)
    square, sum_t, dot_t, f_0, f_1, f_2, ft_0, ft_1 = (zero,) * 8
    for s in stats:
        off = s[0] / (2 * W) - center
        square = square + s[1] + (2 * W) * (off * off)
        sum_t = sum_t + s[2]
        dot_t = dot_t + s[3] + off * s[2]
        f_0 = f_0 + s[4]
        f_1 = f_1 + s[5] + off * s[4]
        f_2 = f_2 + s[6] + 2.0 * off * s[5] + off * off * s[4]
        ft_0 = ft_0 + s[7]
        ft_1 = ft_1 + s[8] + off * s[7]
    inverse = lax.rsqrt(square / D + epsilon)
    mean_t = sum_t / D
    mean_nt = dot_t * inverse / D
    fn_1 = f_1 * inverse
    mean_w = (ft_0 - mean_t * f_0 - mean_nt * fn_1) * inverse / D
    mean_nw = (ft_1 * inverse - mean_t * fn_1 - mean_nt * (f_2 * inverse * inverse)) * inverse / D
    normal = (output - center[None]) * inverse[None]
    weighted = factor * ((tangent - mean_t[None] - normal * mean_nt[None]) * inverse[None])
    cot[:, block] = ((weighted - mean_w[None] - normal * mean_nw[None]) * inverse[None]).astype(bf16)

    cot_slots = gather_start(cot, FAR[::-1])
    back_slot = fresh("recv", 5 * NY)
    grad_slot = fresh("recv", NZ * NY)

    def back_step(n):
        chunk = BACKWARD[n]
        size = len(chunk)
        gather_wait(cot, cot_slots, chunk)
        left, right = stacked(cot.at[0], chunk), stacked(cot.at[1], chunk)
        back_f[pl.ds(0, size * GROUP)] = dot_last(left, w_dn[0]) + dot_last(right, w_dn[1])

        def share(j):
            mine = lax.rem(y + j, NY) * OWN
            return [back_f[pl.ds(pl.multiple_of(i * GROUP + mine, OWN), OWN)] for i in range(size)]

        for j in J_ORDER:
            for i, value in enumerate(share(j)):
                back_s[n, j - 1, i] = value.astype(bf16)
            few = pl.ds(0, size)
            copy_to(back_s.at[n, j - 1, few], back_r.at[n, j - 1, few], at_y(j), back_slot + n * NY + j)
        for i, value in enumerate(share(0)):
            back_own[n, i] = value
        if n == len(BACKWARD) - 1:
            copy_to(cot.at[other], cot_x, sibling, cot_x_slot)

    def grad_step(n):
        chunk = BACKWARD[n]
        few = pl.ds(0, len(chunk))
        for j in range(1, NY):
            arrived(back_r.at[n, j - 1, few], back_slot + n * NY + j)
        for i, offset in enumerate(chunk):
            sums = back_own[n, i]
            for j in range(1, NY):
                sums = sums + back_r[n, j - 1, i].astype(f32)
            rows = share_rows(offset, y)
            grad[rows] = (sums * slope[offset].astype(f32)).astype(bf16)
            for j in J_ORDER:
                copy_to(grad.at[rows], grad.at[rows], at_y(j), grad_slot + offset * NY + j)

    def swap_step(n):
        for offset in BACKWARD[n]:
            for j in range(1, NY):
                arrived(grad.at[share_rows(offset, y - j)], grad_slot + offset * NY + j)
            rows = group(offset)
            copy_to(grad.at[rows], grad_x.at[rows], sibling, grad_x_slot + offset)

    def product(first, first_x, second, second_x, result, slot):
        copies = []
        for n in range(TILES):
            part = pl.ds(n * TILE, TILE)
            stage[slot, part] = dot_first(first(part), second[...]) + dot_first(first_x(part), second_x[...])
            copies.append(copy_here(stage.at[slot, part], result.at[part]))
        return copies

    back_step(0)
    back_step(1)
    back_step(2)
    grad_step(0)
    back_step(3)
    grad_step(1)
    swap_step(0)
    back_step(4)
    grad_step(2)
    swap_step(1)
    grad_step(3)
    arrived(hidden_x, hidden_x_slot)
    arrived(normed_x, normed_x_slot)
    arrived(cot_x, cot_x_slot)
    grad_step(4)
    written = product(
        lambda part: both[0, :, part], lambda part: hidden_x[:, part], cot.at[c], cot_x, down_out, 0,
    )
    swap_step(2)
    swap_step(3)
    swap_step(4)
    for k in range(NZ):
        arrived(grad_x.at[group(k)], grad_x_slot + k)
    written += product(
        lambda part: normed[c, :, part], lambda part: normed_x[:, part], grad, grad_x, up_out, 1,
    )
    for copy in written:
        copy.wait()
    for copy in sends:
        copy.wait_send()
    assert counts["send"] <= N_SEND and counts["recv"] <= N_RECV and counts["local"] <= N_LOCAL


def on_device(*args):
    any_ = pl.BlockSpec(memory_space=pl.ANY)
    vmem = pl.BlockSpec(memory_space=pltpu.VMEM)
    scratch = [
        ((2, W, W), bf16), ((2, W, W), bf16), ((2, W, W), bf16), ((2, W, W), bf16),
        ((2, OWN, W), bf16), ((2, OWN, W), f32), ((W,), f32), ((W,), f32), ((W,), f32),
        ((NY, OWN, 128), f32), ((NY, OWN, 128), f32),
        ((2, ROWS, W), bf16), ((ROWS, W), bf16),
        ((2, 2 * GROUP, W), f32), ((5, 3, 2, 2, OWN, W), bf16), ((5, 3, 2, 2, OWN, W), bf16), ((5, 2, 2, OWN, W), f32),
        ((2, ROWS, W), bf16), ((ROWS, W), bf16), ((NZ, OWN, W), bf16),
        ((2, 2, 2 * GROUP, W), f32), ((2, 2, 2, GROUP, W), bf16), ((2, 2, 2, GROUP, W), bf16),
        ((7, 2, 2, OWN, W), f32), ((7, 3, 2, 2, OWN, W), bf16), ((7, 3, 2, 2, OWN, W), bf16),
        ((7, 2, 2, OWN, W), bf16), ((7, 2, 2, OWN, W), bf16),
        ((2, ROWS, W), bf16), ((ROWS, W), bf16),
        ((2 * GROUP, W), f32), ((5, 3, 2, OWN, W), bf16), ((5, 3, 2, OWN, W), bf16), ((5, 2, OWN, W), f32),
        ((ROWS, W), bf16), ((ROWS, W), bf16), ((2, W, W), f32),
    ]
    return pl.pallas_call(
        kernel,
        out_shape=(jax.ShapeDtypeStruct((W, W), f32), jax.ShapeDtypeStruct((W, W), f32)),
        in_specs=[any_, vmem, vmem, any_, vmem, any_, vmem, any_, any_, any_],
        out_specs=(any_, any_),
        scratch_shapes=[pltpu.VMEM(shape, dtype) for shape, dtype in scratch]
        + [pltpu.SemaphoreType.DMA((N_SEND,)), pltpu.SemaphoreType.DMA((N_RECV,)), pltpu.SemaphoreType.DMA((N_LOCAL,))],
        compiler_params=pltpu.CompilerParams(
            collective_id=0, has_side_effects=True, vmem_limit_bytes=60 * 2**20
        ),
        cost_estimate=pl.CostEstimate(flops=9663676416, bytes_accessed=9437184, transcendentals=262144),
        name="gauss_newton",
    )(*args)


def solution(mesh):
    return jax.shard_map(
        on_device,
        mesh=mesh,
        in_specs=(
            P("dp", "tensor"),
            P("tensor"),
            P("tensor"),
            P("tensor", "dp"),
            P("dp"),
            P("dp", "tensor"),
            P("tensor"),
            P("dp", "tensor"),
            P("tensor", "dp"),
            P("dp", "tensor"),
        ),
        out_specs=(P("tensor", "dp"), P("dp", "tensor")),
        check_vma=False,
    )
```

time: 182 us -> 134 us (0.74)
  Pallas kernels: 177 us -> 128 us
    pallas_call x1, Pallas kernels: 177 us -> 128 us  [on_device(): pl.pallas_call(kernel, out_shape=(jax.ShapeDtypeStruct((W, W), f32), jax....]
where the time goes in v2:
time: 134 us
  Pallas kernels  128 us (96%)
  local copies, waits for them, and re-layouts  4.78 us (4%)
    pallas_call x1, Pallas kernels, on_device(): pl.pallas_call(kernel, out_shape=(jax.ShapeDtypeStruct((W, W), f32), jax....  128 us
    unnamed x4, local copies, waits for them, and re-layouts  4.78 us

profile of v2, /device:TPU:1, one launch (start us, length us, event | category | flops | bytes accessed | tf_op | source)
XLA Modules:
  0.0 133.5 jit_solution(11361423745926263501)
XLA Ops:
  0.6 128.1 %gauss_newton.1 = (f32[768,768]{1,0:T(8,128)}, f32[768,768]{1,0:T(8,128)}) custom-call(bf16[32,768]{1,0:T(8,128)(2,1)} %tokens.1, f32[768]{0:T(1024)} %gain_in.1, f32[768]{0:T(1024)} %shift_in.1, bf16[768,768]{1,0:T(8,128)(2,1)} %up_weight.1, f32[768]{0:T(1024)} %up_bias.1, bf16[768,768]{1,0:T(8,128)(2,1)} %down_weight.1, f32[768]{0:T(1024)} %gain_out.1, ...), custom_call_target="tpu_custom_call" | custom-call | flops 9663676416 | bytes 9437184 | tf_op jit(solution)/shard_map/gauss_newton/pallas_call | solution.py:493
  128.7 0.0 copy-start
  128.8 3.4 %copy.14 = f32[768,768]{1,0:T(8,128)} copy(f32[768,768]{1,0:T(8,128)} %get-tuple-element.4) | data formatting | bytes 4718592
  132.1 0.0 copy-done
  132.1 1.4 %copy.15 = f32[768,768]{1,0:T(8,128)} copy(f32[768,768]{1,0:T(8,128)S(1)} %copy-done) | data formatting | bytes 4718592
Async XLA Ops:
  128.7 3.4 %copy-start = (f32[768,768]{1,0:T(8,128)S(1)}, f32[768,768]{1,0:T(8,128)}, u32[]{:S(2)}) copy-start(f32[768,768]{1,0:T(8,128)} %get-tuple-element.5) | copy-start | bytes 7077892

commit v3 on v2

v3 whole, which is shorter than its diff:
```python
import functools

import jax
import jax.numpy as jnp
from jax import lax
from jax.experimental import pallas as pl
from jax.experimental.pallas import tpu as pltpu
from jax.sharding import PartitionSpec as P

D = 6144
epsilon = 1e-05
root_half = 0.7071067811865476
inv_root_two_pi = 0.3989422804014327

f32 = jnp.float32
bf16 = jnp.bfloat16
MESH = pl.DeviceIdType.MESH

NX, NZ, NY = 4, 8, 4
OWN = 16
GROUP = NX * OWN
ROWS = NZ * GROUP
W = 768
TILE = 256
TILES = W // TILE
FORWARD = {"0": (0,), "4": (4,), "17": (1, 7), "3": (3,), "5": (5,), "2": (2,), "6": (6,)}
BACKWARD = {"0": (0,), "17": (1, 7), "26": (2, 6), "35": (3, 5), "4": (4,)}
NEAR = (1, 7)
FAR = (4, 3, 5, 2, 6)
J_ORDER = (2, 1, 3)

N_SEND = 22
N_RECV = 94
N_LOCAL = 11


def dot(a, b):
    return jnp.dot(a, b, preferred_element_type=f32)


def dot_last(a, b):
    return lax.dot_general(a, b, (((1,), (1,)), ((), ())), preferred_element_type=f32)


def dot_first(a, b):
    return lax.dot_general(a, b, (((0,), (0,)), ((), ())), preferred_element_type=f32)


def columns(values):
    lane = lax.broadcasted_iota(jnp.int32, (OWN, 128), 1)
    out = jnp.zeros((OWN, 128), f32)
    for at, value in enumerate(values):
        out = jnp.where(lane == at, value, out)
    return out


def row_sum(pair):
    return jnp.sum(pair[0] + pair[1], axis=1, keepdims=True)


def kernel(
    tokens, gain_in, shift_in, up_weight, up_bias, down_weight, gain_out, curvature, up_tangent, down_tangent,
    down_out, normed_out, normed_x_out, grad_out, grad_x_out,
    w_up, w_ut, w_dn, w_dt, tok, curv, gin_x, sin_x, gout_x,
    stat_a, stat_b, normed, part_f, part_s, part_r, part_own,
    both, hidden_x, slope, out_f, raw_s, raw_r, own_x, out_s, out_r, sum_s, sum_r,
    cot, cot_x, back_f, back_s, back_r, back_own, grad, stage, w_dn_t,
    send_sem, recv_sem, local_sem,
):
    d, t = lax.axis_index("dp"), lax.axis_index("tensor")
    x, z = d // NZ, lax.rem(d, NZ)
    y, c = t // 2, lax.rem(t, 2)
    other = 1 - c

    def at_x(k):
        return (lax.rem(x + k, NX) * NZ + z, t)

    def at_z(k):
        return (x * NZ + lax.rem(z + k, NZ), t)

    def at_y(k):
        return (d, lax.rem(y + k, NY) * 2 + c)

    sibling = (d, y * 2 + other)
    ends, counts = [], {"send": 0, "recv": 0, "local": 0}

    def fresh(kind, n=1):
        at = counts[kind]
        counts[kind] += n
        return at

    def sends_of(ref):
        slot = fresh("send")
        ends.append((ref, slot))
        return slot

    def copy_to(src, dst, device, sent, slot):
        pltpu.make_async_remote_copy(
            src_ref=src, dst_ref=dst, send_sem=send_sem.at[sent],
            recv_sem=recv_sem.at[slot], device_id=device, device_id_type=MESH,
        ).start()

    def bytes_of(ref, sent, slot):
        return pltpu.make_async_remote_copy(
            src_ref=ref, dst_ref=ref, send_sem=send_sem.at[sent],
            recv_sem=recv_sem.at[slot], device_id=sibling, device_id_type=MESH,
        )

    def arrived(ref, slot):
        bytes_of(ref, 0, slot).wait_recv()

    def copy_here(src, dst):
        copy = pltpu.make_async_copy(src, dst, local_sem.at[fresh("local")])
        copy.start()
        return copy

    own_rows = pl.ds(pl.multiple_of(c * OWN, OWN), OWN)
    their_rows = pl.ds(pl.multiple_of(other * OWN, OWN), OWN)
    tok_here = copy_here(tokens.at[own_rows], tok.at[c])
    curv_here = copy_here(curvature.at[own_rows], curv.at[c])
    up_here = [copy_here(up_weight, w_up.at[c]), copy_here(up_tangent, w_ut.at[c])]
    down_here = [copy_here(down_weight, w_dn.at[c]), copy_here(down_tangent, w_dt.at[c])]
    barrier = pltpu.get_barrier_semaphore()
    peers = [sibling] + [at_x(k) for k in range(1, NX)] + [at_z(k) for k in range(1, NZ)] + [at_y(k) for k in range(1, NY)]
    for peer in peers:
        pl.semaphore_signal(barrier, inc=1, device_id=peer, device_id_type=MESH)
    pl.semaphore_wait(barrier, len(peers))

    tok_slot, params_slot, curv_slot = fresh("recv"), fresh("recv", 3), fresh("recv")
    up_slot, down_slot = fresh("recv"), fresh("recv")
    copy_to(tokens.at[their_rows], tok.at[c], sibling, sends_of(tok.at[c]), tok_slot)
    for i, (mine, theirs) in enumerate(((gain_in, gin_x), (shift_in, sin_x), (gain_out, gout_x))):
        copy_to(mine, theirs, sibling, sends_of(theirs), params_slot + i)

    def send_weights(pairs, whole, slot):
        sent = sends_of(whole)
        for mine, theirs in pairs:
            copy_to(mine, theirs.at[c], sibling, sent, slot)

    tok_here.wait()
    arrived(tok.at[other], tok_slot)
    source = tok[...].astype(f32)
    total = row_sum(source)
    spread = source - (total / (2 * W))[None]
    stat_a[0] = columns([total, row_sum(spread * spread)])
    stat_slot, sent = fresh("recv"), sends_of(stat_a.at[pl.ds(1, 3)])
    for k in J_ORDER:
        copy_to(stat_a.at[0], stat_a.at[k], at_y(k), sent, stat_slot)
    arrived(gin_x, params_slot)
    arrived(sin_x, params_slot + 1)
    arrived(gout_x, params_slot + 2)

    def by_half(mine, theirs):
        mine, theirs = mine[...].reshape(1, W), theirs[...].reshape(1, W)
        first = jnp.where(c == 0, mine, theirs)
        second = jnp.where(c == 0, theirs, mine)
        return jnp.stack([first, second])

    gain, shift = by_half(gain_in, gin_x), by_half(shift_in, sin_x)
    arrived(stat_a.at[pl.ds(1, 3)], stat_slot)
    totals = [stat_a[k][:, 0:1] for k in range(NY)]
    center = (totals[0] + totals[1] + totals[2] + totals[3]) / D
    variance = jnp.zeros_like(center)
    for k in range(NY):
        off = totals[k] / (2 * W) - center
        variance = variance + stat_a[k][:, 1:2] + (2 * W) * (off * off)
    inverse = lax.rsqrt(variance / D + epsilon)
    def group(k):
        return pl.ds(pl.multiple_of(lax.rem(z + NZ + k, NZ) * GROUP, GROUP), GROUP)

    def block_of(j, k):
        first = lax.rem(z + NZ + k, NZ) * GROUP + lax.rem(x + NX + j, NX) * OWN
        return pl.ds(pl.multiple_of(first, OWN), OWN)

    block = block_of(0, 0)
    normed[:, block] = ((source - center[None]) * inverse[None] * gain + shift).astype(bf16)

    def three_of(offset):
        first = lax.rem(z + NZ + offset, NZ) * GROUP
        return pl.ds(pl.multiple_of(first, GROUP), GROUP - OWN)

    def gather_start(array, far, between):
        sent = sends_of(array.at[:, pl.ds(0, ROWS - OWN)])

        def send(rows, device, slot):
            copy_to(array.at[:, rows], array.at[:, rows], device, sent, slot)

        z_slot, x_slot, last_slot = fresh("recv", NZ), fresh("recv", NX), fresh("recv", NZ)
        for j in J_ORDER:
            send(block, at_x(j), x_slot + j)
        for k in NEAR + far:
            send(block, at_z(k), last_slot + k if k in NEAR else z_slot + k)
        between()
        for j in (1, 3, 2):
            rows = block_of(-j, 0)
            arrived(array.at[:, rows], x_slot + j)
            for k in NEAR:
                send(rows, at_z(k), last_slot + k)
        for k in far:
            rows = block_of(0, -k)
            arrived(array.at[:, rows], z_slot + k)
            for j in J_ORDER:
                send(rows, at_x(j), last_slot + k)
        return last_slot

    def gather_wait(array, last_slot, chunk):
        for offset in chunk:
            k = (NZ - offset) % NZ
            if k in NEAR:
                arrived(array.at[:, group(-k)], last_slot + k)
            elif k:
                arrived(array.at[:, three_of(-k)], last_slot + k)

    def stacked(array, chunk):
        parts = [array[group(offset)] for offset in chunk]
        return parts[0] if len(parts) == 1 else jnp.concatenate(parts, axis=0)

    normed_slots = gather_start(
        normed, (3, 5, 4, 2, 6), lambda: send_weights(((up_weight, w_up), (up_tangent, w_ut)), w_up, up_slot)
    )
    send_weights(((down_weight, w_dn), (down_tangent, w_dt)), w_dn, down_slot)
    copy_to(curvature.at[their_rows], curv.at[c], sibling, sends_of(curv.at[c]), curv_slot)

    share_slot, share_sent = fresh("recv", NZ), sends_of(part_s)
    both_slot, both_sent = fresh("recv", NZ), sends_of(both.at[:, pl.ds(0, ROWS - NZ * OWN)])
    normed_x_slot, hidden_x_slot = fresh("recv"), fresh("recv")
    raw_slot, raw_sent = fresh("recv", 2), sends_of(raw_s)
    out_slot, out_sent = fresh("recv", 6), sends_of(out_s)
    sum_slot, sum_sent = fresh("recv"), sends_of(sum_s)
    ordered = (0,) + FAR

    def up_step(name):
        chunk = FORWARD[name]
        size = len(chunk)
        gather_wait(normed, normed_slots, chunk)
        if name == "0":
            for copy in up_here:
                copy.wait()
            arrived(w_up, up_slot)
        left, right = stacked(normed.at[0], chunk), stacked(normed.at[1], chunk)
        rows = pl.ds(0, size * GROUP)
        part_f[0, rows] = dot(left, w_up[0]) + dot(right, w_up[1])
        part_f[1, rows] = dot(left, w_ut[0]) + dot(right, w_ut[1])

        def share(i, j):
            mine = lax.rem(y + j, NY) * OWN
            return part_f[:, pl.ds(pl.multiple_of(i * GROUP + mine, OWN), OWN)]

        for j in J_ORDER:
            for i, offset in enumerate(chunk):
                part_s[offset, j - 1] = share(i, j).astype(bf16)
                copy_to(part_s.at[offset, j - 1], part_r.at[offset, j - 1], at_y(j), share_sent, share_slot + offset)
        for i, offset in enumerate(chunk):
            part_own[offset] = share(i, 0)

    def share_rows(offset, who):
        first = lax.rem(z + offset, NZ) * GROUP + lax.rem(who + NY, NY) * OWN
        return pl.ds(pl.multiple_of(first, OWN), OWN)

    def act_step(name):
        for offset in FORWARD[name]:
            arrived(part_r.at[offset], share_slot + offset)
            sums = part_own[offset]
            for j in range(1, NY):
                sums = sums + part_r[offset, j - 1].astype(f32)
            pre = sums[0] + up_bias[...].reshape(1, W)
            phi = 0.5 * (1.0 + lax.erf(pre * root_half))
            derivative = phi + pre * jnp.exp(-0.5 * pre * pre) * inv_root_two_pi
            rows = share_rows(offset, y)
            both[0, rows] = (pre * phi).astype(bf16)
            both[1, rows] = (derivative * sums[1]).astype(bf16)
            slope[offset] = derivative.astype(bf16)
            for j in J_ORDER:
                copy_to(both.at[:, rows], both.at[:, rows], at_y(j), both_sent, both_slot + offset)

    def down_step(name):
        chunk = FORWARD[name]
        for offset in chunk:
            arrived(both.at[:, three_of(offset)], both_slot + offset)
        if name == "4":
            for copy in down_here:
                copy.wait()
            arrived(w_dn, down_slot)
        hidden, hidden_tangent = stacked(both.at[0], chunk), stacked(both.at[1], chunk)
        rows = pl.ds(0, len(chunk) * GROUP)
        for f in range(2):
            out_f[0, f, rows] = dot(hidden, w_dn[f])
            out_f[1, f, rows] = dot(hidden_tangent, w_dn[f]) + dot(hidden, w_dt[f])
        for i, offset in enumerate(chunk):
            if offset in NEAR:
                at = NEAR.index(offset)
                raw_s[at] = out_f[:, :, pl.ds(i * GROUP, GROUP)].astype(bf16)
                copy_to(raw_s.at[at], raw_r.at[at], at_z(offset), raw_sent, raw_slot + at)
                continue
            at = ordered.index(offset)
            if offset == 0:
                for k in range(len(NEAR)):
                    arrived(raw_r.at[k], raw_slot + k)

            def part(j):
                first = pl.multiple_of(lax.rem(x + j, NX) * OWN, OWN)
                value = out_f[:, :, pl.ds(first, OWN)]
                if offset == 0:
                    for k in range(len(NEAR)):
                        value = value + raw_r[k, :, :, pl.ds(first, OWN)].astype(f32)
                return value

            for j in J_ORDER:
                out_s[at, j - 1] = part(j).astype(bf16)
                copy_to(out_s.at[at, j - 1], out_r.at[at, j - 1], at_x(j), out_sent, out_slot + at)
            own_x[at] = part(0)

    def summed(offset):
        at = ordered.index(offset)
        arrived(out_r.at[at], out_slot + at)
        value = own_x[at]
        for j in range(1, NX):
            value = value + out_r[at, j - 1].astype(f32)
        return value

    def sum_step(name):
        for offset in FORWARD[name]:
            at = FAR.index(offset)
            sum_s[at] = summed(offset).astype(bf16)
            copy_to(sum_s.at[at], sum_r.at[at], at_z(offset), sum_sent, sum_slot)

    steps = {"u": up_step, "a": act_step, "d": down_step, "s": sum_step}
    order = ("u0", "u17", "u5", "u4", "u3", "u6", "a4", "a3", "a6", "a17", "d4", "u2", "d3", "a5", "d6", "d17", "a2", "s4", "d5", "a0", "s3", "d2", "s5", "d0", "s6", "s2")
    for step in order:
        if step == "a2":
            copy_to(normed.at[other], normed_x_out, sibling, sends_of(normed.at[other]), normed_x_slot)
            normed_written = copy_here(normed.at[c], normed_out)
            for f in range(2):
                w_dn_t[f] = w_dn[f].T
        steps[step[0]](step[1:])
    copy_to(both.at[0], hidden_x, sibling, sends_of(both.at[0]), hidden_x_slot)

    arrived(curv.at[other], curv_slot)
    curv_here.wait()
    gain = by_half(gain_out, gout_x)
    factor = gain * gain * curv[...]
    outputs = summed(0)
    arrived(sum_r, sum_slot)
    for k in range(len(FAR)):
        outputs = outputs + sum_r[k].astype(f32)

    output = tok[...].astype(f32) + outputs[0]
    tangent = outputs[1]
    total = row_sum(output)
    around = output - (total / (2 * W))[None]
    factor_around = factor * around
    stat_b[0] = columns([
        total, row_sum(around * around), row_sum(tangent), row_sum(around * tangent),
        row_sum(factor), row_sum(factor_around), row_sum(factor_around * around),
        row_sum(factor * tangent), row_sum(factor_around * tangent),
    ])
    stat_slot, sent = fresh("recv"), sends_of(stat_b.at[pl.ds(1, 3)])
    for k in J_ORDER:
        copy_to(stat_b.at[0], stat_b.at[k], at_y(k), sent, stat_slot)
    arrived(stat_b.at[pl.ds(1, 3)], stat_slot)
    stats = [[stat_b[k][:, i:i + 1] for i in range(9)] for k in range(NY)]
    center = (stats[0][0] + stats[1][0] + stats[2][0] + stats[3][0]) / D
    zero = jnp.zeros_like(center)
    square, sum_t, dot_t, f_0, f_1, f_2, ft_0, ft_1 = (zero,) * 8
    for s in stats:
        off = s[0] / (2 * W) - center
        square = square + s[1] + (2 * W) * (off * off)
        sum_t = sum_t + s[2]
        dot_t = dot_t + s[3] + off * s[2]
        f_0 = f_0 + s[4]
        f_1 = f_1 + s[5] + off * s[4]
        f_2 = f_2 + s[6] + 2.0 * off * s[5] + off * off * s[4]
        ft_0 = ft_0 + s[7]
        ft_1 = ft_1 + s[8] + off * s[7]
    inverse = lax.rsqrt(square / D + epsilon)
    mean_t = sum_t / D
    mean_nt = dot_t * inverse / D
    fn_1 = f_1 * inverse
    mean_w = (ft_0 - mean_t * f_0 - mean_nt * fn_1) * inverse / D
    mean_nw = (ft_1 * inverse - mean_t * fn_1 - mean_nt * (f_2 * inverse * inverse)) * inverse / D
    normal = (output - center[None]) * inverse[None]
    weighted = factor * ((tangent - mean_t[None] - normal * mean_nt[None]) * inverse[None])
    cot[:, block] = ((weighted - mean_w[None] - normal * mean_nw[None]) * inverse[None]).astype(bf16)

    cot_slots = gather_start(cot, FAR[::-1], lambda: None)
    back_slot, back_sent = fresh("recv", NZ), sends_of(back_s)
    grad_slot, grad_sent = fresh("recv", NZ), sends_of(grad.at[pl.ds(0, ROWS - NZ * OWN)])
    cot_x_slot, cot_x_sent = fresh("recv"), sends_of(cot.at[other])
    grad_x_slot, grad_x_sent = fresh("recv"), sends_of(grad)
    grad_written = fresh("local")

    def back_step(name):
        chunk = BACKWARD[name]
        size = len(chunk)
        gather_wait(cot, cot_slots, chunk)
        left, right = stacked(cot.at[0], chunk), stacked(cot.at[1], chunk)
        back_f[pl.ds(0, size * GROUP)] = dot(left, w_dn_t[0]) + dot(right, w_dn_t[1])

        def share(i, j):
            mine = lax.rem(y + j, NY) * OWN
            return back_f[pl.ds(pl.multiple_of(i * GROUP + mine, OWN), OWN)]

        for j in J_ORDER:
            for i, offset in enumerate(chunk):
                back_s[offset, j - 1] = share(i, j).astype(bf16)
                copy_to(back_s.at[offset, j - 1], back_r.at[offset, j - 1], at_y(j), back_sent, back_slot + offset)
        for i, offset in enumerate(chunk):
            back_own[offset] = share(i, 0)
            rows = group(offset)
            copy_to(cot.at[other, rows], cot_x.at[rows], sibling, cot_x_sent, cot_x_slot)

    def grad_step(name):
        for offset in BACKWARD[name]:
            arrived(back_r.at[offset], back_slot + offset)
            sums = back_own[offset]
            for j in range(1, NY):
                sums = sums + back_r[offset, j - 1].astype(f32)
            rows = share_rows(offset, y)
            grad[rows] = (sums * slope[offset].astype(f32)).astype(bf16)
            for j in J_ORDER:
                copy_to(grad.at[rows], grad.at[rows], at_y(j), grad_sent, grad_slot + offset)

    def swap_step(name):
        for offset in BACKWARD[name]:
            arrived(grad.at[three_of(offset)], grad_slot + offset)
            rows = group(offset)
            copy_to(grad.at[rows], grad_x_out.at[rows], sibling, grad_x_sent, grad_x_slot)
            copy = pltpu.make_async_copy(grad.at[rows], grad_out.at[rows], local_sem.at[grad_written])
            copy.start()

    steps = {"b": back_step, "g": grad_step, "w": swap_step}
    for step in ("b0", "b17", "g0", "b26", "g17", "b35", "b4", "g26", "g35", "g4", "w0", "w17", "w26"):
        steps[step[0]](step[1:])
    arrived(hidden_x, hidden_x_slot)
    arrived(cot_x, cot_x_slot)
    written = [normed_written]
    for n in range(TILES):
        part = pl.ds(n * TILE, TILE)
        stage[part] = dot_first(both[0, :, part], cot[c]) + dot_first(hidden_x[:, part], cot_x[...])
        written.append(copy_here(stage.at[part], down_out.at[part]))
    swap_step("35")
    swap_step("4")
    arrived(normed_x_out, normed_x_slot)
    for copy in written:
        copy.wait()
    for ref, slot in ends:
        bytes_of(ref, slot, 0).wait_send()
    pltpu.make_async_copy(grad, grad_out, local_sem.at[grad_written]).wait()
    arrived(grad_x_out, grad_x_slot)
    assert counts["send"] <= N_SEND and counts["recv"] <= N_RECV and counts["local"] <= N_LOCAL


def finish_kernel(down, normed, normed_x, grad, grad_x, up_out, down_out, n_own, n_x, g_own, g_x, moving, stage, sems):
    pairs = ((normed, n_own), (grad, g_own), (normed_x, n_x), (grad_x, g_x), (down, moving))
    loads = [pltpu.make_async_copy(src, dst, sems.at[i]) for i, (src, dst) in enumerate(pairs)]
    for copy in loads:
        copy.start()
    for copy in loads[:2]:
        copy.wait()
    for n in range(TILES):
        part = pl.ds(n * TILE, TILE)
        stage[part] = dot_first(n_own[:, part], g_own[...])
    for copy in loads[2:]:
        copy.wait()
    moved = pltpu.make_async_copy(moving, down_out, sems.at[0])
    moved.start()
    written = [moved]
    for n in range(TILES):
        part = pl.ds(n * TILE, TILE)
        stage[part] += dot_first(n_x[:, part], g_x[...])
        copy = pltpu.make_async_copy(stage.at[part], up_out.at[part], sems.at[5 + n])
        copy.start()
        written.append(copy)
    for copy in written:
        copy.wait()


def on_device(*args):
    any_ = pl.BlockSpec(memory_space=pl.ANY)
    vmem = pl.BlockSpec(memory_space=pltpu.VMEM)
    scratch = [
        ((2, W, W), bf16), ((2, W, W), bf16), ((2, W, W), bf16), ((2, W, W), bf16),
        ((2, OWN, W), bf16), ((2, OWN, W), f32), ((W,), f32), ((W,), f32), ((W,), f32),
        ((NY, OWN, 128), f32), ((NY, OWN, 128), f32),
        ((2, ROWS, W), bf16),
        ((2, 2 * GROUP, W), f32), ((NZ, 3, 2, OWN, W), bf16), ((NZ, 3, 2, OWN, W), bf16), ((NZ, 2, OWN, W), f32),
        ((2, ROWS, W), bf16), ((ROWS, W), bf16), ((NZ, OWN, W), bf16),
        ((2, 2, 2 * GROUP, W), f32), ((2, 2, 2, GROUP, W), bf16), ((2, 2, 2, GROUP, W), bf16),
        ((6, 2, 2, OWN, W), f32), ((6, 3, 2, 2, OWN, W), bf16), ((6, 3, 2, 2, OWN, W), bf16),
        ((5, 2, 2, OWN, W), bf16), ((5, 2, 2, OWN, W), bf16),
        ((2, ROWS, W), bf16), ((ROWS, W), bf16),
        ((2 * GROUP, W), f32), ((NZ, 3, OWN, W), bf16), ((NZ, 3, OWN, W), bf16), ((NZ, OWN, W), f32),
        ((ROWS, W), bf16), ((W, W), f32), ((2, W, W), bf16),
    ]
    product = jax.ShapeDtypeStruct((W, W), f32)
    rows = jax.ShapeDtypeStruct((ROWS, W), bf16)
    partial = pl.pallas_call(
        kernel,
        out_shape=(product, rows, rows, rows, rows),
        in_specs=[any_, vmem, vmem, any_, vmem, any_, vmem, any_, any_, any_],
        out_specs=(any_,) * 5,
        scratch_shapes=[pltpu.VMEM(shape, dtype) for shape, dtype in scratch]
        + [pltpu.SemaphoreType.DMA((N_SEND,)), pltpu.SemaphoreType.DMA((N_RECV,)), pltpu.SemaphoreType.DMA((N_LOCAL,))],
        compiler_params=pltpu.CompilerParams(
            collective_id=0, has_side_effects=True, vmem_limit_bytes=60 * 2**20
        ),
        cost_estimate=pl.CostEstimate(flops=9663676416, bytes_accessed=9437184, transcendentals=262144),
        name="gauss_newton",
    )(*args)
    return pl.pallas_call(
        finish_kernel,
        out_shape=(product, product),
        in_specs=[any_] * 5,
        out_specs=(any_, any_),
        scratch_shapes=[pltpu.VMEM((ROWS, W), bf16)] * 4
        + [pltpu.VMEM((W, W), f32)] * 2
        + [pltpu.SemaphoreType.DMA((8,))],
        compiler_params=pltpu.CompilerParams(vmem_limit_bytes=60 * 2**20),
        cost_estimate=pl.CostEstimate(flops=1207959552, bytes_accessed=10223616, transcendentals=0),
        name="finish",
    )(*partial)


def solution(mesh):
    return jax.shard_map(
        on_device,
        mesh=mesh,
        in_specs=(
            P("dp", "tensor"),
            P("tensor"),
            P("tensor"),
            P("tensor", "dp"),
            P("dp"),
            P("dp", "tensor"),
            P("tensor"),
            P("dp", "tensor"),
            P("tensor", "dp"),
            P("dp", "tensor"),
        ),
        out_specs=(P("tensor", "dp"), P("dp", "tensor")),
        check_vma=False,
    )
```

time: 134 us -> 126 us (0.940)
  local copies, waits for them, and re-layouts: 4.78 us -> 0 us
  Pallas kernels: 128 us -> 125 us
    unnamed x4 -> x0, local copies, waits for them, and re-layouts: 4.78 us -> none
    pallas_call x1 -> x2, Pallas kernels: 128 us -> 125 us  [the longest x1 120 us: on_device(): pl.pallas_call(kernel, out_shape=(product, rows, rows, rows, rows), in_sp...]
where the time goes in v3:
time: 126 us
  Pallas kernels  125 us (99%)
    pallas_call x1, Pallas kernels, on_device(): pl.pallas_call(kernel, out_shape=(product, rows, rows, rows, rows), in_sp...  120 us
    pallas_call x1, Pallas kernels, on_device(): pl.pallas_call(finish_kernel, out_shape=(product, product), in_specs=[any...  4.87 us

profile of v3, /device:TPU:1, one launch (start us, length us, event | category | flops | bytes accessed | tf_op | source)
XLA Modules:
  0.0 125.7 jit_solution(3486470120996241439)
XLA Ops:
  0.6 120.0 %gauss_newton.1 = (f32[768,768]{1,0:T(8,128)}, bf16[512,768]{1,0:T(8,128)(2,1)}, bf16[512,768]{1,0:T(8,128)(2,1)}, bf16[512,768]{1,0:T(8,128)(2,1)}, bf16[512,768]{1,0:T(8,128)(2,1)}) custom-call(bf16[32,768]{1,0:T(8,128)(2,1)} %tokens.1, f32[768]{0:T(1024)} %gain_in.1, f32[768]{0:T(1024)} %shift_in.1, bf16[768,768]{1,0:T(8,128)(2,1)} %up_weight.1, ...), custom_call_target="tpu_custom_call" | custom-call | flops 9663676416 | bytes 9437184 | tf_op jit(solution)/shard_map/gauss_newton/pallas_call | solution.py:497
  120.6 4.9 %finish.1 = (f32[768,768]{1,0:T(8,128)}, f32[768,768]{1,0:T(8,128)}) custom-call(f32[768,768]{1,0:T(8,128)} %get-tuple-element.7.down, bf16[512,768]{1,0:T(8,128)(2,1)} %get-tuple-element.8.normed, bf16[512,768]{1,0:T(8,128)(2,1)} %get-tuple-element.9.normed_x, bf16[512,768]{1,0:T(8,128)(2,1)} %get-tuple-element.10.grad, ...), custom_call_target="tpu_custom_call" | custom-call | flops 1207959552 | bytes 10223616 | tf_op jit(solution)/shard_map/finish/pallas_call | solution.py:510

commit v4 on v3

--- a/solution.py
+++ b/solution.py
@@ -216,7 +216,7 @@
         return parts[0] if len(parts) == 1 else jnp.concatenate(parts, axis=0)
 
     normed_slots = gather_start(
-        normed, (3, 5, 4, 2, 6), lambda: send_weights(((up_weight, w_up), (up_tangent, w_ut)), w_up, up_slot)
+        normed, (4, 3, 5, 2, 6), lambda: send_weights(((up_weight, w_up), (up_tangent, w_ut)), w_up, up_slot)
     )
     send_weights(((down_weight, w_dn), (down_tangent, w_dt)), w_dn, down_slot)
     copy_to(curvature.at[their_rows], curv.at[c], sibling, sends_of(curv.at[c]), curv_slot)
@@ -233,9 +233,9 @@
         chunk = FORWARD[name]
         size = len(chunk)
         gather_wait(normed, normed_slots, chunk)
-        if name == "0":
-            for copy in up_here:
-                copy.wait()
+        if up_here:
+            while up_here:
+                up_here.pop().wait()
             arrived(w_up, up_slot)
         left, right = stacked(normed.at[0], chunk), stacked(normed.at[1], chunk)
         rows = pl.ds(0, size * GROUP)
@@ -277,9 +277,9 @@
         chunk = FORWARD[name]
         for offset in chunk:
             arrived(both.at[:, three_of(offset)], both_slot + offset)
-        if name == "4":
-            for copy in down_here:
-                copy.wait()
+        if down_here:
+            while down_here:
+                down_here.pop().wait()
             arrived(w_dn, down_slot)
         hidden, hidden_tangent = stacked(both.at[0], chunk), stacked(both.at[1], chunk)
         rows = pl.ds(0, len(chunk) * GROUP)
@@ -325,9 +325,12 @@
             copy_to(sum_s.at[at], sum_r.at[at], at_z(offset), sum_sent, sum_slot)
 
     steps = {"u": up_step, "a": act_step, "d": down_step, "s": sum_step}
-    order = ("u0", "u17", "u5", "u4", "u3", "u6", "a4", "a3", "a6", "a17", "d4", "u2", "d3", "a5", "d6", "d17", "a2", "s4", "d5", "a0", "s3", "d2", "s5", "d0", "s6", "s2")
+    order = (
+        "u0", "u17", "u4", "u3", "a17", "a4", "u5", "a3", "d17", "d4", "u2", "a5", "d3",
+        "u6", "a2", "d5", "s4", "a6", "s3", "a0", "d2", "s5", "d6", "s2", "d0", "s6",
+    )
     for step in order:
-        if step == "a2":
+        if step == "d2":
             copy_to(normed.at[other], normed_x_out, sibling, sends_of(normed.at[other]), normed_x_slot)
             normed_written = copy_here(normed.at[c], normed_out)
             for f in range(2):

time: 126 us -> 120 us (0.952)
  Pallas kernels: 125 us -> 120 us
    pallas_call x1, Pallas kernels: 120 us -> 115 us  [on_device(): pl.pallas_call(kernel, out_shape=(product, rows, rows, rows, rows), in_sp...]
where the time goes in v4:
time: 120 us
  Pallas kernels  120 us (100%)
    pallas_call x1, Pallas kernels, on_device(): pl.pallas_call(kernel, out_shape=(product, rows, rows, rows, rows), in_sp...  115 us
    pallas_call x1, Pallas kernels, on_device(): pl.pallas_call(finish_kernel, out_shape=(product, product), in_specs=[any...  4.87 us

profile of v4, /device:TPU:1, one launch (start us, length us, event | category | flops | bytes accessed | tf_op | source)
XLA Modules:
  0.0 120.3 jit_solution(10900180783728275226)
XLA Ops:
  0.6 114.6 %gauss_newton.1 = (f32[768,768]{1,0:T(8,128)}, bf16[512,768]{1,0:T(8,128)(2,1)}, bf16[512,768]{1,0:T(8,128)(2,1)}, bf16[512,768]{1,0:T(8,128)(2,1)}, bf16[512,768]{1,0:T(8,128)(2,1)}) custom-call(bf16[32,768]{1,0:T(8,128)(2,1)} %tokens.1, f32[768]{0:T(1024)} %gain_in.1, f32[768]{0:T(1024)} %shift_in.1, bf16[768,768]{1,0:T(8,128)(2,1)} %up_weight.1, ...), custom_call_target="tpu_custom_call" | custom-call | flops 9663676416 | bytes 9437184 | tf_op jit(solution)/shard_map/gauss_newton/pallas_call | solution.py:500
  115.3 4.9 %finish.1 = (f32[768,768]{1,0:T(8,128)}, f32[768,768]{1,0:T(8,128)}) custom-call(f32[768,768]{1,0:T(8,128)} %get-tuple-element.7.down, bf16[512,768]{1,0:T(8,128)(2,1)} %get-tuple-element.8.normed, bf16[512,768]{1,0:T(8,128)(2,1)} %get-tuple-element.9.normed_x, bf16[512,768]{1,0:T(8,128)(2,1)} %get-tuple-element.10.grad, ...), custom_call_target="tpu_custom_call" | custom-call | flops 1207959552 | bytes 10223616 | tf_op jit(solution)/shard_map/finish/pallas_call | solution.py:513

commit v5 on v4

--- a/solution.py
+++ b/solution.py
@@ -24,7 +24,7 @@
 TILE = 256
 TILES = W // TILE
 FORWARD = {"0": (0,), "4": (4,), "17": (1, 7), "3": (3,), "5": (5,), "2": (2,), "6": (6,)}
-BACKWARD = {"0": (0,), "17": (1, 7), "26": (2, 6), "35": (3, 5), "4": (4,)}
+BACKWARD = {"0": (0,), "17": (1, 7), "6": (6,), "2": (2,), "5": (5,), "3": (3,), "4": (4,)}
 NEAR = (1, 7)
 FAR = (4, 3, 5, 2, 6)
 J_ORDER = (2, 1, 3)
@@ -179,7 +179,7 @@
         first = lax.rem(z + NZ + offset, NZ) * GROUP
         return pl.ds(pl.multiple_of(first, GROUP), GROUP - OWN)
 
-    def gather_start(array, far, between):
+    def gather_start(array, far, between, relay):
         sent = sends_of(array.at[:, pl.ds(0, ROWS - OWN)])
 
         def send(rows, device, slot):
@@ -188,9 +188,14 @@
         z_slot, x_slot, last_slot = fresh("recv", NZ), fresh("recv", NX), fresh("recv", NZ)
         for j in J_ORDER:
             send(block, at_x(j), x_slot + j)
-        for k in NEAR + far:
-            send(block, at_z(k), last_slot + k if k in NEAR else z_slot + k)
+        for k in (4,) + NEAR if relay else NEAR + far:
+            send(block, at_z(k), z_slot + k)
         between()
+        for k, onward in ((1, ((1, 2), (2, 3))), (7, ((7, 6), (6, 5)))):
+            rows = block_of(0, -k)
+            arrived(array.at[:, rows], z_slot + k)
+            for step, total in onward if relay else ():
+                send(rows, at_z(step), z_slot + total)
         for j in (1, 3, 2):
             rows = block_of(-j, 0)
             arrived(array.at[:, rows], x_slot + j)
@@ -207,7 +212,7 @@
         for offset in chunk:
             k = (NZ - offset) % NZ
             if k in NEAR:
-                arrived(array.at[:, group(-k)], last_slot + k)
+                arrived(array.at[:, three_of(-k)], last_slot + k)
             elif k:
                 arrived(array.at[:, three_of(-k)], last_slot + k)
 
@@ -216,7 +221,7 @@
         return parts[0] if len(parts) == 1 else jnp.concatenate(parts, axis=0)
 
     normed_slots = gather_start(
-        normed, (4, 3, 5, 2, 6), lambda: send_weights(((up_weight, w_up), (up_tangent, w_ut)), w_up, up_slot)
+        normed, (4, 3, 5, 2, 6), lambda: send_weights(((up_weight, w_up), (up_tangent, w_ut)), w_up, up_slot), True
     )
     send_weights(((down_weight, w_dn), (down_tangent, w_dt)), w_dn, down_slot)
     copy_to(curvature.at[their_rows], curv.at[c], sibling, sends_of(curv.at[c]), curv_slot)
@@ -385,7 +390,7 @@
     weighted = factor * ((tangent - mean_t[None] - normal * mean_nt[None]) * inverse[None])
     cot[:, block] = ((weighted - mean_w[None] - normal * mean_nw[None]) * inverse[None]).astype(bf16)
 
-    cot_slots = gather_start(cot, FAR[::-1], lambda: None)
+    cot_slots = gather_start(cot, FAR[::-1], lambda: None, False)
     back_slot, back_sent = fresh("recv", NZ), sends_of(back_s)
     grad_slot, grad_sent = fresh("recv", NZ), sends_of(grad.at[pl.ds(0, ROWS - NZ * OWN)])
     cot_x_slot, cot_x_sent = fresh("recv"), sends_of(cot.at[other])
@@ -431,18 +436,23 @@
             copy = pltpu.make_async_copy(grad.at[rows], grad_out.at[rows], local_sem.at[grad_written])
             copy.start()
 
-    steps = {"b": back_step, "g": grad_step, "w": swap_step}
-    for step in ("b0", "b17", "g0", "b26", "g17", "b35", "b4", "g26", "g35", "g4", "w0", "w17", "w26"):
+    written = [normed_written]
+
+    def product_step(_):
+        arrived(hidden_x, hidden_x_slot)
+        arrived(cot_x, cot_x_slot)
+        for n in range(TILES):
+            part = pl.ds(n * TILE, TILE)
+            stage[part] = dot_first(both[0, :, part], cot[c]) + dot_first(hidden_x[:, part], cot_x[...])
+            written.append(copy_here(stage.at[part], down_out.at[part]))
+
+    steps = {"b": back_step, "g": grad_step, "w": swap_step, "p": product_step}
+    order = (
+        "b0", "b17", "b6", "g0", "b2", "g17", "b5", "g6", "b3", "g2", "b4", "g5",
+        "g3", "g4", "w0", "w17", "w6", "p", "w2", "w5", "w3", "w4",
+    )
+    for step in order:
         steps[step[0]](step[1:])
-    arrived(hidden_x, hidden_x_slot)
-    arrived(cot_x, cot_x_slot)
-    written = [normed_written]
-    for n in range(TILES):
-        part = pl.ds(n * TILE, TILE)
-        stage[part] = dot_first(both[0, :, part], cot[c]) + dot_first(hidden_x[:, part], cot_x[...])
-        written.append(copy_here(stage.at[part], down_out.at[part]))
-    swap_step("35")
-    swap_step("4")
     arrived(normed_x_out, normed_x_slot)
     for copy in written:
         copy.wait()

time: 120 us -> 121 us (level)
  no operation moved by 1% of the time
where the time goes in v5:
time: 121 us; the launch traced here: 120 us
  Pallas kernels  120 us (99%)
    pallas_call x1, Pallas kernels, on_device(): pl.pallas_call(kernel, out_shape=(product, rows, rows, rows, rows), in_sp...  115 us
    pallas_call x1, Pallas kernels, on_device(): pl.pallas_call(finish_kernel, out_shape=(product, product), in_specs=[any...  4.87 us

profile of v5, /device:TPU:1, one launch (start us, length us, event | category | flops | bytes accessed | tf_op | source)
XLA Modules:
  0.0 120.5 jit_solution(15543804057887805458)
XLA Ops:
  0.6 114.8 %gauss_newton.1 = (f32[768,768]{1,0:T(8,128)}, bf16[512,768]{1,0:T(8,128)(2,1)}, bf16[512,768]{1,0:T(8,128)(2,1)}, bf16[512,768]{1,0:T(8,128)(2,1)}, bf16[512,768]{1,0:T(8,128)(2,1)}) custom-call(bf16[32,768]{1,0:T(8,128)(2,1)} %tokens.1, f32[768]{0:T(1024)} %gain_in.1, f32[768]{0:T(1024)} %shift_in.1, bf16[768,768]{1,0:T(8,128)(2,1)} %up_weight.1, ...), custom_call_target="tpu_custom_call" | custom-call | flops 9663676416 | bytes 9437184 | tf_op jit(solution)/shard_map/gauss_newton/pallas_call | solution.py:510
  115.4 4.9 %finish.1 = (f32[768,768]{1,0:T(8,128)}, f32[768,768]{1,0:T(8,128)}) custom-call(f32[768,768]{1,0:T(8,128)} %get-tuple-element.7.down, bf16[512,768]{1,0:T(8,128)(2,1)} %get-tuple-element.8.normed, bf16[512,768]{1,0:T(8,128)(2,1)} %get-tuple-element.9.normed_x, bf16[512,768]{1,0:T(8,128)(2,1)} %get-tuple-element.10.grad, ...), custom_call_target="tpu_custom_call" | custom-call | flops 1207959552 | bytes 10223616 | tf_op jit(solution)/shard_map/finish/pallas_call | solution.py:523

commit v6 on v5

--- a/solution.py
+++ b/solution.py
@@ -31,7 +31,7 @@
 
 N_SEND = 22
 N_RECV = 94
-N_LOCAL = 11
+N_LOCAL = 15
 
 
 def dot(a, b):
@@ -59,12 +59,13 @@
 
 
 def kernel(
-    tokens, gain_in, shift_in, up_weight, up_bias, down_weight, gain_out, curvature, up_tangent, down_tangent,
+    tokens, gain_in_at, shift_in_at, up_weight, up_bias_at, down_weight, gain_out_at, curvature, up_tangent, down_tangent,
     down_out, normed_out, normed_x_out, grad_out, grad_x_out,
     w_up, w_ut, w_dn, w_dt, tok, curv, gin_x, sin_x, gout_x,
     stat_a, stat_b, normed, part_f, part_s, part_r, part_own,
     both, hidden_x, slope, out_f, raw_s, raw_r, own_x, out_s, out_r, sum_s, sum_r,
     cot, cot_x, back_f, back_s, back_r, back_own, grad, stage, w_dn_t,
+    gain_in, shift_in, gain_out, up_bias,
     send_sem, recv_sem, local_sem,
 ):
     d, t = lax.axis_index("dp"), lax.axis_index("tensor")
@@ -114,21 +115,25 @@
         copy.start()
         return copy
 
-    own_rows = pl.ds(pl.multiple_of(c * OWN, OWN), OWN)
-    their_rows = pl.ds(pl.multiple_of(other * OWN, OWN), OWN)
-    tok_here = copy_here(tokens.at[own_rows], tok.at[c])
-    curv_here = copy_here(curvature.at[own_rows], curv.at[c])
-    up_here = [copy_here(up_weight, w_up.at[c]), copy_here(up_tangent, w_ut.at[c])]
-    down_here = [copy_here(down_weight, w_dn.at[c]), copy_here(down_tangent, w_dt.at[c])]
     barrier = pltpu.get_barrier_semaphore()
     peers = [sibling] + [at_x(k) for k in range(1, NX)] + [at_z(k) for k in range(1, NZ)] + [at_y(k) for k in range(1, NY)]
     for peer in peers:
         pl.semaphore_signal(barrier, inc=1, device_id=peer, device_id_type=MESH)
+    own_rows = pl.ds(pl.multiple_of(c * OWN, OWN), OWN)
+    their_rows = pl.ds(pl.multiple_of(other * OWN, OWN), OWN)
+    tok_here = copy_here(tokens.at[own_rows], tok.at[c])
+    vectors = ((gain_in_at, gain_in), (shift_in_at, shift_in), (gain_out_at, gain_out), (up_bias_at, up_bias))
+    vectors_here = [copy_here(src, dst) for src, dst in vectors]
+    curv_here = copy_here(curvature.at[own_rows], curv.at[c])
+    up_here = [copy_here(up_weight, w_up.at[c]), copy_here(up_tangent, w_ut.at[c])]
+    down_here = [copy_here(down_weight, w_dn.at[c]), copy_here(down_tangent, w_dt.at[c])]
     pl.semaphore_wait(barrier, len(peers))
 
     tok_slot, params_slot, curv_slot = fresh("recv"), fresh("recv", 3), fresh("recv")
     up_slot, down_slot = fresh("recv"), fresh("recv")
     copy_to(tokens.at[their_rows], tok.at[c], sibling, sends_of(tok.at[c]), tok_slot)
+    for copy in vectors_here:
+        copy.wait()
     for i, (mine, theirs) in enumerate(((gain_in, gin_x), (shift_in, sin_x), (gain_out, gout_x))):
         copy_to(mine, theirs, sibling, sends_of(theirs), params_slot + i)
 
@@ -490,7 +495,6 @@
 
 def on_device(*args):
     any_ = pl.BlockSpec(memory_space=pl.ANY)
-    vmem = pl.BlockSpec(memory_space=pltpu.VMEM)
     scratch = [
         ((2, W, W), bf16), ((2, W, W), bf16), ((2, W, W), bf16), ((2, W, W), bf16),
         ((2, OWN, W), bf16), ((2, OWN, W), f32), ((W,), f32), ((W,), f32), ((W,), f32),
@@ -504,13 +508,14 @@
         ((2, ROWS, W), bf16), ((ROWS, W), bf16),
         ((2 * GROUP, W), f32), ((NZ, 3, OWN, W), bf16), ((NZ, 3, OWN, W), bf16), ((NZ, OWN, W), f32),
         ((ROWS, W), bf16), ((W, W), f32), ((2, W, W), bf16),
+        ((W,), f32), ((W,), f32), ((W,), f32), ((W,), f32),
     ]
     product = jax.ShapeDtypeStruct((W, W), f32)
     rows = jax.ShapeDtypeStruct((ROWS, W), bf16)
     partial = pl.pallas_call(
         kernel,
         out_shape=(product, rows, rows, rows, rows),
-        in_specs=[any_, vmem, vmem, any_, vmem, any_, vmem, any_, any_, any_],
+        in_specs=[any_] * 10,
         out_specs=(any_,) * 5,
         scratch_shapes=[pltpu.VMEM(shape, dtype) for shape, dtype in scratch]
         + [pltpu.SemaphoreType.DMA((N_SEND,)), pltpu.SemaphoreType.DMA((N_RECV,)), pltpu.SemaphoreType.DMA((N_LOCAL,))],

time: 121 us -> 119 us (0.983)
  Pallas kernels: 120 us -> 118 us
where the time goes in v6:
time: 119 us
  Pallas kernels  118 us (99%)
    pallas_call x1, Pallas kernels, on_device(): pl.pallas_call(kernel, out_shape=(product, rows, rows, rows, rows), in_sp...  114 us
    pallas_call x1, Pallas kernels, on_device(): pl.pallas_call(finish_kernel, out_shape=(product, product), in_specs=[any...  4.87 us

profile of v6, /device:TPU:1, one launch (start us, length us, event | category | flops | bytes accessed | tf_op | source)
XLA Modules:
  0.0 119.3 jit_solution(12383535697282129768)
XLA Ops:
  0.6 113.6 %gauss_newton.1 = (f32[768,768]{1,0:T(8,128)}, bf16[512,768]{1,0:T(8,128)(2,1)}, bf16[512,768]{1,0:T(8,128)(2,1)}, bf16[512,768]{1,0:T(8,128)(2,1)}, bf16[512,768]{1,0:T(8,128)(2,1)}) custom-call(bf16[32,768]{1,0:T(8,128)(2,1)} %tokens.1, f32[768]{0:T(1024)} %gain_in_at.1, f32[768]{0:T(1024)} %shift_in_at.1, bf16[768,768]{1,0:T(8,128)(2,1)} %up_weight.1, ...), custom_call_target="tpu_custom_call" | custom-call | flops 9663676416 | bytes 9437184 | tf_op jit(solution)/shard_map/gauss_newton/pallas_call | solution.py:515
  114.3 4.9 %finish.1 = (f32[768,768]{1,0:T(8,128)}, f32[768,768]{1,0:T(8,128)}) custom-call(f32[768,768]{1,0:T(8,128)} %get-tuple-element.7.down, bf16[512,768]{1,0:T(8,128)(2,1)} %get-tuple-element.8.normed, bf16[512,768]{1,0:T(8,128)(2,1)} %get-tuple-element.9.normed_x, bf16[512,768]{1,0:T(8,128)(2,1)} %get-tuple-element.10.grad, ...), custom_call_target="tpu_custom_call" | custom-call | flops 1207959552 | bytes 10223616 | tf_op jit(solution)/shard_map/finish/pallas_call | solution.py:528
